TPU v7x, 32 devices: a whole 2x2x4 slice. The times are simulated.
32 devices in a mesh: ctx: 16 (over z, y, x), dp: 2 (over core).
Axes of the slice: x: 2, y: 2, z: 4, core: 2. Of those that a mesh axis runs over, the one named last changes fastest.
Arguments:
- layer_input: bfloat16 [4, 1024, 4096], P('dp', 'ctx'), may hold values from -0.5 to 0.5
- queries: bfloat16 [4, 1024, 1024], P('dp', 'ctx'), may hold values from -8 to 8
- key_states: bfloat16 [4, 1024, 128], P('dp', 'ctx'), may hold values from -8 to 8
- value_states: bfloat16 [4, 1024, 128], P('dp', 'ctx'), may hold values from -6 to 6
- attn_output: bfloat16 [4, 1024, 1024], P('dp', 'ctx'), may hold values from -6 to 6
- out_grad: bfloat16 [4, 1024, 1024], P('dp', 'ctx'), may hold values from -6 to 6
- doc_ids: int32 [4, 1024], P('dp'), may hold values from 0 to 7, never falling along the last dimension, each value on 1 to 256 neighbouring positions
- positions: int32 [4, 1024], P('dp'), may hold values from 0 to 1023, as said below
Outputs:
- query_grad: bfloat16 [4, 1024, 1024], P('dp', 'ctx')
- kv_weight_grad: float32 [4096, 256], P('ctx')
Inputs may be any that keep to these rules, and one draw needn't show every extreme that they name: `positions`: stored row c * 64 + r of a sequence (c below 16, r below 64) holds a position from r * (16) to (r + 1) * 16 - 1; every position of a sequence is held by exactly one row.
All inputs are finite; a program needn't handle non-finite values.
Results may differ from a plain program's by a relative error of at most 0.005.
Values may be sent and summed in bfloat16 or wider, within the bound.
A program may use at most 64 MiB of HBM per device.

v0:
```python
import math

import jax
import jax.numpy as jnp
from jax import lax
from jax.sharding import PartitionSpec as P

NEG_FILL = -1e30


def passed_along(x, axis, by):
    length = lax.axis_size(axis)
    return lax.ppermute(x, axis, [(i, (i + by) % length) for i in range(length)])


def heads_first(tensor, head_count):
    seq_count, row_count, width_all = tensor.shape
    head_size = width_all // head_count
    split_up = tensor.reshape(seq_count, row_count, head_count, head_size)
    return split_up.transpose(0, 2, 1, 3).reshape(seq_count, head_count * row_count, head_size)


def local(
    layer_input, queries, key_states, value_states, attn_output, out_grad, doc_ids, positions
):
    seq_count, row_count, model_width = layer_input.shape
    head_size = key_states.shape[2]
    head_count = queries.shape[2] // head_size
    ctx_count = lax.axis_size("ctx")
    ctx_index = lax.axis_index("ctx")
    score_scale = 1.0 / math.sqrt(head_size)
    query_n = heads_first(queries, head_count)
    grad_n = heads_first(out_grad, head_count)
    row_product = (out_grad.astype(jnp.float32) * attn_output.astype(jnp.float32)).reshape(
        seq_count, row_count, head_count, head_size
    )
    delta_n = (
        jnp.sum(row_product, axis=3).transpose(0, 2, 1).reshape(seq_count, head_count * row_count)
    )
    doc_full = jnp.take_along_axis(doc_ids, positions, axis=1)
    own_pos = lax.dynamic_slice_in_dim(positions, ctx_index * row_count, row_count, 1)
    own_doc = lax.dynamic_slice_in_dim(doc_full, ctx_index * row_count, row_count, 1)
    query_pos = jnp.tile(own_pos, (1, head_count))
    query_doc = jnp.tile(own_doc, (1, head_count))
    key_all, value_all = (
        lax.all_gather(key_states, "ctx", axis=1, tiled=True),
        lax.all_gather(value_states, "ctx", axis=1, tiled=True),
    )
    group_rows = 4 * row_count
    query_total = head_count * row_count

    def live_mask(key_doc, key_pos):
        return (key_doc[:, :, None] == query_doc[:, None, :]) & (
            key_pos[:, :, None] <= query_pos[:, None, :]
        )

    def scores_of(key_block):
        return (
            jnp.einsum("skd,snd->skn", key_block, query_n, preferred_element_type=jnp.float32)
            * score_scale
        )

    def stats_step(group_index, loop_state):
        run_max, run_sum = loop_state
        row_start = group_index * group_rows
        key_block = lax.dynamic_slice_in_dim(key_all, row_start, group_rows, 1)
        key_doc = lax.dynamic_slice_in_dim(doc_full, row_start, group_rows, 1)
        key_pos = lax.dynamic_slice_in_dim(positions, row_start, group_rows, 1)
        live_pairs = live_mask(key_doc, key_pos)
        scores = scores_of(key_block)
        block_max = jnp.max(jnp.where(live_pairs, scores, NEG_FILL), axis=1)
        new_max = jnp.maximum(run_max, block_max)
        exp_terms = jnp.where(live_pairs, jnp.exp(scores - new_max[:, None, :]), 0.0)
        run_sum = run_sum * jnp.exp(run_max - new_max) + jnp.sum(exp_terms, axis=1)
        return (new_max, run_sum)

    start_max = jnp.full((seq_count, query_total), NEG_FILL, jnp.float32)
    start_sum = jnp.zeros((seq_count, query_total), jnp.float32)
    run_max, run_sum = lax.fori_loop(0, ctx_count // 4, stats_step, (start_max, start_sum))
    log_total = run_max + jnp.log(run_sum)

    def block_terms(row_start, block_rows):
        key_block = lax.dynamic_slice_in_dim(key_all, row_start, block_rows, 1)
        value_block = lax.dynamic_slice_in_dim(value_all, row_start, block_rows, 1)
        key_doc = lax.dynamic_slice_in_dim(doc_full, row_start, block_rows, 1)
        key_pos = lax.dynamic_slice_in_dim(positions, row_start, block_rows, 1)
        live_pairs = live_mask(key_doc, key_pos)
        scores = scores_of(key_block)
        probs = jnp.where(live_pairs, jnp.exp(scores - log_total[:, None, :]), 0.0)
        probs_half = probs.astype(jnp.bfloat16)
        value_grad = jnp.einsum(
            "skn,snd->skd", probs_half, grad_n, preferred_element_type=jnp.float32
        )
        prob_grad = jnp.einsum(
            "skd,snd->skn", value_block, grad_n, preferred_element_type=jnp.float32
        )
        score_grad = (probs * (prob_grad - delta_n[:, None, :])).astype(jnp.bfloat16)
        query_part = jnp.einsum(
            "skn,skd->snd", score_grad, key_block, preferred_element_type=jnp.float32
        )
        key_grad = (
            jnp.einsum("skn,snd->skd", score_grad, query_n, preferred_element_type=jnp.float32)
            * score_scale
        )
        return (jnp.concatenate([key_grad, value_grad], axis=2), query_part)

    start_query = jnp.zeros((seq_count, query_total, head_size), jnp.float32)

    def pass_on(accumulated):
        return passed_along(accumulated, "ctx", 1)

    def one_block(accumulated, query_sum, step_index):
        block_index = (ctx_index - step_index - 1) % ctx_count
        partial_value, query_part = block_terms(block_index * row_count, row_count)
        return (accumulated + partial_value, query_sum + query_part)

    def four_steps(turn_index, loop_state):
        accumulated, query_sum = loop_state
        for inner_step in range(4):
            accumulated, query_sum = one_block(accumulated, query_sum, 4 * turn_index + inner_step)
            accumulated = pass_on(accumulated)
        return (accumulated, query_sum)

    start_accum = jnp.zeros((seq_count, row_count, 2 * head_size), jnp.float32)
    accumulated, query_sum = lax.fori_loop(
        0, ctx_count // 4 - 1, four_steps, (start_accum, start_query)
    )
    for inner_step in range(3):
        accumulated, query_sum = one_block(accumulated, query_sum, ctx_count - 4 + inner_step)
        accumulated = pass_on(accumulated)
    accumulated, query_sum = one_block(accumulated, query_sum, ctx_count - 1)
    query_grad = (query_sum * score_scale).reshape(seq_count, head_count, row_count, head_size)
    query_grad = (
        query_grad.transpose(0, 2, 1, 3)
        .reshape(seq_count, row_count, head_count * head_size)
        .astype(jnp.bfloat16)
    )
    kv_half = accumulated.astype(jnp.bfloat16)
    flat_input = layer_input.reshape(seq_count * row_count, model_width)
    flat_grad = kv_half.reshape(seq_count * row_count, 2 * head_size)
    row_share = lax.psum_scatter(
        lax.dot_general(
            flat_input, flat_grad, (((0,), (0,)), ((), ())), preferred_element_type=jnp.float32
        ),
        "ctx",
        scatter_dimension=0,
        tiled=True,
    )
    weight_grad = lax.psum(row_share, "dp")
    return (query_grad, weight_grad)


def solution(mesh):
    in_specs = (
        P("dp", "ctx", None),
        P("dp", "ctx", None),
        P("dp", "ctx", None),
        P("dp", "ctx", None),
        P("dp", "ctx", None),
        P("dp", "ctx", None),
        P("dp", None),
        P("dp", None),
    )
    out_specs = (P("dp", "ctx", None), P("ctx", None))
    return jax.shard_map(local, mesh=mesh, in_specs=in_specs, out_specs=out_specs, check_vma=False)
```

profile of v0, /device:TPU:0, one launch (start us, length us, event | category | flops | bytes accessed | tf_op | source)
XLA Modules:
  0.0 396.5 jit_solution(7671687622956216244)
XLA Ops:
  7.3 1.0 copy_bitcast_fusion.1
  8.3 1.1 convert_multiply_fusion
  10.8 17.7 %gather_fusion = s32[2048]{0:T(1024)S(1)} fusion(s32[2,1024]{1,0:T(2,128)S(1)} %copy-done.1, s32[2048]{0:T(1024)S(1)} %bitcast.180), kind=kCustom, calls=%fused_computation | custom fusion | bytes 32768 | tf_op jit(solution)/shard_map/jit(take_along_axis)/gather | solution.py:40
  28.9 47.9 %all_gather.6 = bf16[2,1024,128]{2,1,0:T(8,128)(2,1)} all-gather(bf16[2,64,128]{2,1,0:T(8,128)(2,1)S(1)} %copy-done.5), channel_id=1, replica_groups=mesh['ctx'=16,'dp'=2] {'ctx'}, dimensions={1}, use_global_device_ids=true | all-gather | bytes 557056 | tf_op jit(solution)/shard_map/all_gather | solution.py:46
  76.8 7.5 %while.36 = (s32[]{:T(128)}, f32[2,512]{1,0:T(2,128)S(1)}, f32[2,512]{1,0:T(2,128)S(1)}, s32[2,1024]{1,0:T(2,128)S(1)}, s32[2,1024]{1,0:T(2,128)S(1)}, /*index=5...) while((s32[]{:T(128)}, f32[2,512]{1,0:T(2,128)S(1)}, ...), condition=%wide.region_3.4_spmd.clone, body=%wide.region_0.3_spmd.clone.sunk | while | flops 70259720 | bytes 2602182 | solution.py:79
  77.0 1.3 select_reduce_fusion.4
  78.9 1.3 select_reduce_fusion.4
  80.7 1.3 select_reduce_fusion.4
  82.6 1.3 select_reduce_fusion.4
  84.3 40.6 %all_gather.7 = bf16[2,1024,128]{2,1,0:T(8,128)(2,1)} all-gather(bf16[2,64,128]{2,1,0:T(8,128)(2,1)S(1)} %copy-done.6), channel_id=1, replica_groups=mesh['ctx'=16,'dp'=2] {'ctx'}, dimensions={1}, use_global_device_ids=true | all-gather | bytes 557056 | tf_op jit(solution)/shard_map/all_gather | solution.py:47
  125.0 1.0 fusion.78
  126.2 1.0 fusion.82
  127.3 120.5 %while.37 = (s32[]{:T(128)}, f32[2,64,256]{2,1,0:T(8,128)S(1)}, f32[2,512,128]{2,1,0:T(8,128)S(1)}, s32[]{:T(128)}, s32[2,1024]{1,0:T(2,128)S(1)}, /*index=5*/s3...) while((s32[]{:T(128)}, f32[2,64,256]{2,1,0:T(8,128)S(1)}, ...), condition=%wide.wide.region_6.7_spmd.clone, body=%wide.wide.region_5.6_spmd.clone.sunk | while | flops 339148864 | bytes 17799372 | solution.py:125
  127.7 1.0 fusion.324
  130.1 2.1 collective-permute-start
  132.2 1.0 fusion.333
  134.4 1.0 fusion.330
  135.6 1.0 fusion.332
  136.5 1.0 fusion.327
  138.7 1.0 convolution_add_fusion.16
  139.8 1.0 convolution_add_fusion.17
  140.8 1.0 convolution_add_fusion.18
  142.4 9.2 %collective-permute-done.1 = f32[2,64,256]{2,1,0:T(8,128)S(1)} collective-permute-done((f32[2,64,256]{2,1,0:T(8,128)S(1)}, f32[2,64,256]{2,1,0:T(8,128)S(1)}, u32[]{:S(2)}, u32[]{:S(2)}) %collective-permute-start.1) | collective-permute-done | bytes 131104 | tf_op jit(solution)/shard_map/while/body/eval_jaxpr/ppermute | solution.py:13
  151.8 8.6 %collective-permute-done.2 = f32[2,64,256]{2,1,0:T(8,128)S(1)} collective-permute-done((f32[2,64,256]{2,1,0:T(8,128)S(1)}, f32[2,64,256]{2,1,0:T(8,128)S(1)}, u32[]{:S(2)}, u32[]{:S(2)}) %collective-permute-start.2) | collective-permute-done | bytes 131104 | tf_op jit(solution)/shard_map/while/body/eval_jaxpr/ppermute | solution.py:13
  160.4 1.0 convolution_add_fusion.19
  161.5 7.5 %collective-permute-done.3 = f32[2,64,256]{2,1,0:T(8,128)S(1)} collective-permute-done((f32[2,64,256]{2,1,0:T(8,128)S(1)}, f32[2,64,256]{2,1,0:T(8,128)S(1)}, u32[]{:S(2)}, u32[]{:S(2)}) %collective-permute-start.3) | collective-permute-done | bytes 131104 | tf_op jit(solution)/shard_map/while/body/eval_jaxpr/ppermute | solution.py:13
  169.2 1.0 fusion.324
  171.7 1.0 fusion.333
  173.9 1.0 fusion.330
  176.0 1.0 fusion.327
  178.2 1.0 convolution_add_fusion.16
  179.2 1.0 convolution_add_fusion.17
  180.3 1.0 convolution_add_fusion.18
  181.8 8.4 %collective-permute-done.1 = f32[2,64,256]{2,1,0:T(8,128)S(1)} collective-permute-done((f32[2,64,256]{2,1,0:T(8,128)S(1)}, f32[2,64,256]{2,1,0:T(8,128)S(1)}, u32[]{:S(2)}, u32[]{:S(2)}) %collective-permute-start.1) | collective-permute-done | bytes 131104 | tf_op jit(solution)/shard_map/while/body/eval_jaxpr/ppermute | solution.py:13
  190.5 8.4 %collective-permute-done.2 = f32[2,64,256]{2,1,0:T(8,128)S(1)} collective-permute-done((f32[2,64,256]{2,1,0:T(8,128)S(1)}, f32[2,64,256]{2,1,0:T(8,128)S(1)}, u32[]{:S(2)}, u32[]{:S(2)}) %collective-permute-start.2) | collective-permute-done | bytes 131104 | tf_op jit(solution)/shard_map/while/body/eval_jaxpr/ppermute | solution.py:13
  198.9 1.0 convolution_add_fusion.19
  200.0 7.8 %collective-permute-done.3 = f32[2,64,256]{2,1,0:T(8,128)S(1)} collective-permute-done((f32[2,64,256]{2,1,0:T(8,128)S(1)}, f32[2,64,256]{2,1,0:T(8,128)S(1)}, u32[]{:S(2)}, u32[]{:S(2)}) %collective-permute-start.3) | collective-permute-done | bytes 131104 | tf_op jit(solution)/shard_map/while/body/eval_jaxpr/ppermute | solution.py:13
  208.0 1.0 fusion.324
  210.4 1.0 fusion.333
  212.6 1.0 fusion.330
  214.8 1.0 fusion.327
  216.9 1.0 convolution_add_fusion.16
  218.0 1.0 convolution_add_fusion.17
  219.1 1.0 convolution_add_fusion.18
  220.6 9.5 %collective-permute-done.1 = f32[2,64,256]{2,1,0:T(8,128)S(1)} collective-permute-done((f32[2,64,256]{2,1,0:T(8,128)S(1)}, f32[2,64,256]{2,1,0:T(8,128)S(1)}, u32[]{:S(2)}, u32[]{:S(2)}) %collective-permute-start.1) | collective-permute-done | bytes 131104 | tf_op jit(solution)/shard_map/while/body/eval_jaxpr/ppermute | solution.py:13
  230.3 8.9 %collective-permute-done.2 = f32[2,64,256]{2,1,0:T(8,128)S(1)} collective-permute-done((f32[2,64,256]{2,1,0:T(8,128)S(1)}, f32[2,64,256]{2,1,0:T(8,128)S(1)}, u32[]{:S(2)}, u32[]{:S(2)}) %collective-permute-start.2) | collective-permute-done | bytes 131104 | tf_op jit(solution)/shard_map/while/body/eval_jaxpr/ppermute | solution.py:13
  239.3 1.0 convolution_add_fusion.19
  240.4 7.5 %collective-permute-done.3 = f32[2,64,256]{2,1,0:T(8,128)S(1)} collective-permute-done((f32[2,64,256]{2,1,0:T(8,128)S(1)}, f32[2,64,256]{2,1,0:T(8,128)S(1)}, u32[]{:S(2)}, u32[]{:S(2)}) %collective-permute-start.3) | collective-permute-done | bytes 131104 | tf_op jit(solution)/shard_map/while/body/eval_jaxpr/ppermute | solution.py:13
  248.0 1.0 fusion.79
  250.1 1.0 fusion.80
  251.3 1.0 fusion.84
  252.3 1.0 fusion.81
  253.5 1.0 fusion.85
  254.7 1.9 collective-permute-done.4
  256.8 8.4 %collective-permute-done.5 = f32[2,64,256]{2,1,0:T(8,128)S(1)} collective-permute-done((f32[2,64,256]{2,1,0:T(8,128)S(1)}, f32[2,64,256]{2,1,0:T(8,128)S(1)}, u32[]{:S(2)}, u32[]{:S(2)}) %collective-permute-start.5) | collective-permute-done | bytes 131104 | tf_op jit(solution)/shard_map/ppermute | solution.py:13
  265.4 8.4 %collective-permute-done.6 = f32[2,64,256]{2,1,0:T(8,128)S(1)} collective-permute-done((f32[2,64,256]{2,1,0:T(8,128)S(1)}, f32[2,64,256]{2,1,0:T(8,128)S(1)}, u32[]{:S(2)}, u32[]{:S(2)}) %collective-permute-start.6) | collective-permute-done | bytes 131104 | tf_op jit(solution)/shard_map/ppermute | solution.py:13
  273.8 2.7 convolution_bitcast_fusion
  276.6 1.0 convolution_add_fusion.7
  277.6 1.1 convolution_add_fusion.6
  278.7 89.0 %reduce-scatter.2.cloned.1.call-done = f32[256,256]{0,1:T(8,128)} async-done(((f32[4096,256]{0,1:T(8,128)}), f32[256,256]{0,1:T(8,128)}) %reduce-scatter.2.cloned.1.call-update) | async-done | bytes 262160 | tf_op jit(solution)/shard_map/reduce_scatter | solution.py:141
  367.7 1.0 convolution_add_fusion.5
  368.8 1.1 fusion.65
  370.6 17.3 %all-reduce.2.cloned.1.call-done = f32[256,256]{0,1:T(8,128)} async-done(((f32[256,256]{0,1:T(8,128)}), f32[256,256]{0,1:T(8,128)}) %all-reduce.2.cloned.1.call-update) | async-done | bytes 262160 | tf_op jit(solution)/shard_map/psum | solution.py:149
  387.9 1.8 copy.28
  (166 shorter events, 23.8 us)
Async XLA Ops:
  7.2 266.6 %copy-start = (bf16[2,64,4096]{2,1,0:T(8,128)(2,1)S(1)}, bf16[2,64,4096]{2,1,0:T(8,128)(2,1)}, u32[]{:S(2)}) copy-start(bf16[2,64,4096]{2,1,0:T(8,128)(2,1)} %param.12) | copy-start | bytes 3145732
  7.2 3.5 copy-start.1
  7.2 360.5 %reduce-scatter.2.cloned.1.call-start = ((), (), s32[]{:S(2)}) async-start(), calls=%async_computation.1 | async-start | bytes 4456448 | tf_op jit(solution)/shard_map/reduce_scatter | solution.py:141
  9.8 18.6 %copy-start.4 = (f32[2,8,64]{2,1,0:T(8,128)}, f32[2,8,64]{2,1,0:T(8,128)S(1)}, u32[]{:S(2)}) copy-start(f32[2,8,64]{2,1,0:T(8,128)S(1)} %copy.25) | copy-start | bytes 12292
  10.7 17.8 %copy-start.2 = (s32[2,1024]{1,0:T(2,128)S(1)}, s32[2,1024]{1,0:T(2,128)}, u32[]{:S(2)}) copy-start(s32[2,1024]{1,0:T(2,128)} %param.19) | copy-start | bytes 24580
  10.7 18.1 %copy-start.3 = (bf16[2,64,1024]{2,1,0:T(8,128)(2,1)S(1)}, bf16[2,64,1024]{2,1,0:T(8,128)(2,1)}, u32[]{:S(2)}) copy-start(bf16[2,64,1024]{2,1,0:T(8,128)(2,1)} %param.13) | copy-start | bytes 786436
  10.7 18.1 %copy-start.5 = (bf16[2,64,128]{2,1,0:T(8,128)(2,1)S(1)}, bf16[2,64,128]{2,1,0:T(8,128)(2,1)}, u32[]{:S(2)}) copy-start(bf16[2,64,128]{2,1,0:T(8,128)(2,1)} %param.14) | copy-start | bytes 98308
  76.8 7.5 %copy-start.6 = (bf16[2,64,128]{2,1,0:T(8,128)(2,1)S(1)}, bf16[2,64,128]{2,1,0:T(8,128)(2,1)}, u32[]{:S(2)}) copy-start(bf16[2,64,128]{2,1,0:T(8,128)(2,1)} %param.15) | copy-start | bytes 98308
  130.1 12.0 %collective-permute-start = (f32[2,64,256]{2,1,0:T(8,128)S(1)}, f32[2,64,256]{2,1,0:T(8,128)S(1)}, u32[]{:S(2)}, u32[]{:S(2)}) collective-permute-start(f32[2,64,256]{2,1,0:T(8,128)S(1)} %maximum_add_fusion.16), channel_id=1, source_target_pairs={{0,2},{2,4},{4,6},{6,8},{8,10},{10,12},{12,14},{14,16},{16,18},{18... | collective-permute-start | bytes 393224 | tf_op jit(solution)/shard_map/while/body/eval_jaxpr/ppermute | solution.py:13
  142.1 9.4 %collective-permute-start.1 = (f32[2,64,256]{2,1,0:T(8,128)S(1)}, f32[2,64,256]{2,1,0:T(8,128)S(1)}, u32[]{:S(2)}, u32[]{:S(2)}) collective-permute-start(f32[2,64,256]{2,1,0:T(8,128)S(1)} %maximum_add_fusion.17), channel_id=1, source_target_pairs={{0,2},{2,4},{4,6},{6,8},{8,10},{10,12},{12,14},{14,16},{16,18},{18... | collective-permute-start | bytes 393224 | tf_op jit(solution)/shard_map/while/body/eval_jaxpr/ppermute | solution.py:13
  151.5 8.8 %collective-permute-start.2 = (f32[2,64,256]{2,1,0:T(8,128)S(1)}, f32[2,64,256]{2,1,0:T(8,128)S(1)}, u32[]{:S(2)}, u32[]{:S(2)}) collective-permute-start(f32[2,64,256]{2,1,0:T(8,128)S(1)} %maximum_add_fusion.18), channel_id=1, source_target_pairs={{0,2},{2,4},{4,6},{6,8},{8,10},{10,12},{12,14},{14,16},{16,18},{18... | collective-permute-start | bytes 393224 | tf_op jit(solution)/shard_map/while/body/eval_jaxpr/ppermute | solution.py:13
  160.4 8.6 %collective-permute-start.3 = (f32[2,64,256]{2,1,0:T(8,128)S(1)}, f32[2,64,256]{2,1,0:T(8,128)S(1)}, u32[]{:S(2)}, u32[]{:S(2)}) collective-permute-start(f32[2,64,256]{2,1,0:T(8,128)S(1)} %maximum_add_fusion.19), channel_id=1, source_target_pairs={{0,2},{2,4},{4,6},{6,8},{8,10},{10,12},{12,14},{14,16},{16,18},{18... | collective-permute-start | bytes 393224 | tf_op jit(solution)/shard_map/while/body/eval_jaxpr/ppermute | solution.py:13
  171.6 9.9 %collective-permute-start = (f32[2,64,256]{2,1,0:T(8,128)S(1)}, f32[2,64,256]{2,1,0:T(8,128)S(1)}, u32[]{:S(2)}, u32[]{:S(2)}) collective-permute-start(f32[2,64,256]{2,1,0:T(8,128)S(1)} %maximum_add_fusion.16), channel_id=1, source_target_pairs={{0,2},{2,4},{4,6},{6,8},{8,10},{10,12},{12,14},{14,16},{16,18},{18... | collective-permute-start | bytes 393224 | tf_op jit(solution)/shard_map/while/body/eval_jaxpr/ppermute | solution.py:13
  181.6 8.6 %collective-permute-start.1 = (f32[2,64,256]{2,1,0:T(8,128)S(1)}, f32[2,64,256]{2,1,0:T(8,128)S(1)}, u32[]{:S(2)}, u32[]{:S(2)}) collective-permute-start(f32[2,64,256]{2,1,0:T(8,128)S(1)} %maximum_add_fusion.17), channel_id=1, source_target_pairs={{0,2},{2,4},{4,6},{6,8},{8,10},{10,12},{12,14},{14,16},{16,18},{18... | collective-permute-start | bytes 393224 | tf_op jit(solution)/shard_map/while/body/eval_jaxpr/ppermute | solution.py:13
  190.2 8.6 %collective-permute-start.2 = (f32[2,64,256]{2,1,0:T(8,128)S(1)}, f32[2,64,256]{2,1,0:T(8,128)S(1)}, u32[]{:S(2)}, u32[]{:S(2)}) collective-permute-start(f32[2,64,256]{2,1,0:T(8,128)S(1)} %maximum_add_fusion.18), channel_id=1, source_target_pairs={{0,2},{2,4},{4,6},{6,8},{8,10},{10,12},{12,14},{14,16},{16,18},{18... | collective-permute-start | bytes 393224 | tf_op jit(solution)/shard_map/while/body/eval_jaxpr/ppermute | solution.py:13
  198.9 8.9 %collective-permute-start.3 = (f32[2,64,256]{2,1,0:T(8,128)S(1)}, f32[2,64,256]{2,1,0:T(8,128)S(1)}, u32[]{:S(2)}, u32[]{:S(2)}) collective-permute-start(f32[2,64,256]{2,1,0:T(8,128)S(1)} %maximum_add_fusion.19), channel_id=1, source_target_pairs={{0,2},{2,4},{4,6},{6,8},{8,10},{10,12},{12,14},{14,16},{16,18},{18... | collective-permute-start | bytes 393224 | tf_op jit(solution)/shard_map/while/body/eval_jaxpr/ppermute | solution.py:13
  210.4 9.9 %collective-permute-start = (f32[2,64,256]{2,1,0:T(8,128)S(1)}, f32[2,64,256]{2,1,0:T(8,128)S(1)}, u32[]{:S(2)}, u32[]{:S(2)}) collective-permute-start(f32[2,64,256]{2,1,0:T(8,128)S(1)} %maximum_add_fusion.16), channel_id=1, source_target_pairs={{0,2},{2,4},{4,6},{6,8},{8,10},{10,12},{12,14},{14,16},{16,18},{18... | collective-permute-start | bytes 393224 | tf_op jit(solution)/shard_map/while/body/eval_jaxpr/ppermute | solution.py:13
  220.3 9.7 %collective-permute-start.1 = (f32[2,64,256]{2,1,0:T(8,128)S(1)}, f32[2,64,256]{2,1,0:T(8,128)S(1)}, u32[]{:S(2)}, u32[]{:S(2)}) collective-permute-start(f32[2,64,256]{2,1,0:T(8,128)S(1)} %maximum_add_fusion.17), channel_id=1, source_target_pairs={{0,2},{2,4},{4,6},{6,8},{8,10},{10,12},{12,14},{14,16},{16,18},{18... | collective-permute-start | bytes 393224 | tf_op jit(solution)/shard_map/while/body/eval_jaxpr/ppermute | solution.py:13
  230.1 9.2 %collective-permute-start.2 = (f32[2,64,256]{2,1,0:T(8,128)S(1)}, f32[2,64,256]{2,1,0:T(8,128)S(1)}, u32[]{:S(2)}, u32[]{:S(2)}) collective-permute-start(f32[2,64,256]{2,1,0:T(8,128)S(1)} %maximum_add_fusion.18), channel_id=1, source_target_pairs={{0,2},{2,4},{4,6},{6,8},{8,10},{10,12},{12,14},{14,16},{16,18},{18... | collective-permute-start | bytes 393224 | tf_op jit(solution)/shard_map/while/body/eval_jaxpr/ppermute | solution.py:13
  239.3 8.6 %collective-permute-start.3 = (f32[2,64,256]{2,1,0:T(8,128)S(1)}, f32[2,64,256]{2,1,0:T(8,128)S(1)}, u32[]{:S(2)}, u32[]{:S(2)}) collective-permute-start(f32[2,64,256]{2,1,0:T(8,128)S(1)} %maximum_add_fusion.19), channel_id=1, source_target_pairs={{0,2},{2,4},{4,6},{6,8},{8,10},{10,12},{12,14},{14,16},{16,18},{18... | collective-permute-start | bytes 393224 | tf_op jit(solution)/shard_map/while/body/eval_jaxpr/ppermute | solution.py:13
  247.9 8.6 %collective-permute-start.4 = (f32[2,64,256]{2,1,0:T(8,128)S(1)}, f32[2,64,256]{2,1,0:T(8,128)S(1)}, u32[]{:S(2)}, u32[]{:S(2)}) collective-permute-start(f32[2,64,256]{2,1,0:T(8,128)S(1)} %maximum_add_fusion.4), channel_id=1, source_target_pairs={{0,2},{2,4},{4,6},{6,8},{8,10},{10,12},{12,14},{14,16},{16,18},{18... | collective-permute-start | bytes 393224 | tf_op jit(solution)/shard_map/ppermute | solution.py:13
  256.5 8.6 %collective-permute-start.5 = (f32[2,64,256]{2,1,0:T(8,128)S(1)}, f32[2,64,256]{2,1,0:T(8,128)S(1)}, u32[]{:S(2)}, u32[]{:S(2)}) collective-permute-start(f32[2,64,256]{2,1,0:T(8,128)S(1)} %maximum_add_fusion.5), channel_id=1, source_target_pairs={{0,2},{2,4},{4,6},{6,8},{8,10},{10,12},{12,14},{14,16},{16,18},{18... | collective-permute-start | bytes 393224 | tf_op jit(solution)/shard_map/ppermute | solution.py:13
  265.2 8.6 %collective-permute-start.6 = (f32[2,64,256]{2,1,0:T(8,128)S(1)}, f32[2,64,256]{2,1,0:T(8,128)S(1)}, u32[]{:S(2)}, u32[]{:S(2)}) collective-permute-start(f32[2,64,256]{2,1,0:T(8,128)S(1)} %maximum_add_fusion.6), channel_id=1, source_target_pairs={{0,2},{2,4},{4,6},{6,8},{8,10},{10,12},{12,14},{14,16},{16,18},{18... | collective-permute-start | bytes 393224 | tf_op jit(solution)/shard_map/ppermute | solution.py:13
  276.5 111.3 %all-reduce.2.cloned.1.call-start = ((), (), s32[]{:S(2)}) async-start(), calls=%async_computation.2 | async-start | bytes 524288 | tf_op jit(solution)/shard_map/psum | solution.py:149
Sparse Core Ops, SparseCore 0:
  276.6 90.9 reduce-scatter.1
  370.0 17.8 all-reduce.1
where the time goes:
time: 400 us; the launch traced here: 396 us
  waiting for transfers between devices  200 us (50%)
  blocking collectives  88.6 us (22%)
  matrix products  61.9 us (15%)
  local copies, waits for them, and re-layouts  23.4 us (6%)
  between operations  14.5 us (4%)
    ppermute x15, waiting for transfers between devices, passed_along(): lax.ppermute(x, axis, [(i, (i + by) % length) for i in range(length)])  94.2 us
    reduce_scatter x1, waiting for transfers between devices, local(): lax.psum_scatter(lax.dot_general(flat_input, flat_grad, (((0,), (0,)), ((...  89 us
    all_gather x1, blocking collectives, local(): lax.all_gather(key_states, 'ctx', axis=1, tiled=True)  47.9 us
    all_gather x1, blocking collectives, local(): lax.all_gather(value_states, 'ctx', axis=1, tiled=True)  40.6 us
    dot_general x20, matrix products, scores_of(): jnp.einsum('skd,snd->skn', key_block, query_n, preferred_element_type=jnp...  21.1 us
    gather x2, local copies, waits for them, and re-layouts, local(): doc_full = jnp.take_along_axis(doc_ids, positions, axis=1)  17.7 us
    psum x1, waiting for transfers between devices, local(): weight_grad = lax.psum(row_share, 'dp')  17.3 us
    dot_general x16, matrix products, block_terms(): jnp.einsum('skn,skd->snd', score_grad, key_block, preferred_element_type=...  16.8 us
  transfers between devices with their start and end apart: 17, of which 14 were waited for; matrix products, arithmetic and copies ran while one was open for 11% of the time, Pallas kernels for 0%

commit v1 on v0

v1 whole, which is shorter than its diff:
```python
import functools
import math

import jax
import jax.numpy as jnp
from jax import lax
from jax.experimental import pallas as pl
from jax.experimental.pallas import tpu as pltpu
from jax.sharding import PartitionSpec as P

NEG_FILL = -1e30
INNER = 4
LANES = 128


def kernel(
    dims,
    x_ref,
    q_ref,
    k_ref,
    v_ref,
    a_ref,
    g_ref,
    doc_ref,
    pos_ref,
    dq_ref,
    dw_ref,
    kv,
    kpos,
    dcol,
    acc,
    plane_out,
    plane_in,
    plane_sum,
    outer_out,
    outer_in,
    kvg,
    xg,
    wsum,
    w_out,
    w_in,
    w_fin,
    ag_send,
    ag_recv,
    plane_send,
    plane_recv,
    outer_send,
    outer_recv,
    kvg_send,
    kvg_recv,
    x_send,
    x_recv,
    w_send,
    w_recv,
    fin_send,
    fin_recv,
    own_sem,
):
    outer, pairs, width = dims
    seqs, rows, head = k_ref.shape
    heads = q_ref.shape[2] // head
    groups = 4
    step = rows // groups
    lanes_n = heads * step
    scale = 1.0 / math.sqrt(head)
    x_parts = xg.shape[1] if x_ref.ndim == 2 else 1

    me = lax.axis_index("ctx")
    pair = lax.axis_index("dp")
    o_me, i_me = me // INNER, me % INNER

    def inner_of(k):
        low = (i_me % 2 + k % 2) % 2
        high = (i_me // 2 + k // 2) % 2
        return high * 2 + low

    def outer_of(m):
        return (o_me + m) % outer

    def ctx_of(o, i):
        return o * INNER + i

    def copy_to(src, dst, send_sem, recv_sem, ctx, dp):
        return pltpu.make_async_remote_copy(
            src_ref=src,
            dst_ref=dst,
            send_sem=send_sem,
            recv_sem=recv_sem,
            device_id={"ctx": ctx, "dp": dp},
            device_id_type=pl.DeviceIdType.MESH,
        )

    pending = []

    def start(copy):
        copy.start()
        pending.append(copy)

    slots = [(k, e) for k in range(INNER) for e in range(pairs)]

    barrier = pltpu.get_barrier_semaphore()
    greeted = 0
    for m in range(1, outer):
        pl.semaphore_signal(
            barrier,
            inc=1,
            device_id={"ctx": ctx_of(outer_of(m), i_me), "dp": pair},
            device_id_type=pl.DeviceIdType.MESH,
        )
        greeted += 1
    for k, e in slots[1:]:
        pl.semaphore_signal(
            barrier,
            inc=1,
            device_id={"ctx": ctx_of(o_me, inner_of(k)), "dp": (pair + e) % pairs},
            device_id_type=pl.DeviceIdType.MESH,
        )
        greeted += 1
    for s in range(seqs):
        kv[s, me, :, 0:head] = k_ref[s]
        kv[s, me, :, head : 2 * head] = v_ref[s]
    pl.semaphore_wait(barrier, greeted)

    for s in range(seqs):
        for m in range(1, outer):
            start(
                copy_to(
                    kv.at[s, me],
                    kv.at[s, me],
                    ag_send.at[s, m - 1],
                    ag_recv.at[s, me],
                    ctx_of(outer_of(m), i_me),
                    pair,
                )
            )
        for k in range(1, INNER):
            start(
                copy_to(
                    kv.at[s, me],
                    kv.at[s, me],
                    ag_send.at[s, outer - 1 + k - 1],
                    ag_recv.at[s, me],
                    ctx_of(o_me, inner_of(k)),
                    pair,
                )
            )

    def arrived(s, src):
        copy_to(
            kv.at[s, src], kv.at[s, src], ag_send.at[s, 0], ag_recv.at[s, src], me, pair
        ).wait_recv()

    def forward(s):
        for m in range(1, outer):
            src = ctx_of(outer_of(outer - m), i_me)
            arrived(s, src)
            for k in range(1, INNER):
                start(
                    copy_to(
                        kv.at[s, src],
                        kv.at[s, src],
                        ag_send.at[s, outer - 1 + 3 * m + k - 1],
                        ag_recv.at[s, src],
                        ctx_of(o_me, inner_of(k)),
                        pair,
                    )
                )

    def columns_of(row):
        return jnp.broadcast_to(row, (LANES, LANES)).T

    def query_rows(s):
        total = kpos.shape[1] * rows
        per = LANES // rows
        for b in range(total // LANES):
            cut = slice(b * LANES, (b + 1) * LANES)
            pos_col = columns_of(pos_ref[s : s + 1, cut].astype(jnp.float32))
            kpos[s, b * per : (b + 1) * per] = pos_col.reshape(per, rows, LANES)
            dcol[s, cut] = columns_of(doc_ref[s : s + 1, cut].astype(jnp.float32))
        doc_cols = dcol[s]
        place = lax.broadcasted_iota(jnp.int32, (total, LANES), 0).astype(jnp.float32)
        sub = lax.broadcasted_iota(jnp.int32, (step, LANES), 0)
        lane = lax.broadcasted_iota(jnp.int32, (step, LANES), 1)
        pick = sub == lane % step
        found = []
        for g in range(groups):
            own = kpos[s, me, g * step : (g + 1) * step, :]
            pos = jnp.sum(jnp.where(pick, own, 0.0), axis=0, keepdims=True)
            doc = jnp.sum(jnp.where(place == pos, doc_cols, 0.0), axis=0, keepdims=True)
            first = jnp.sum(jnp.where(doc_cols < doc, 1.0, 0.0), axis=0, keepdims=True)
            product = heads_of(g_ref, s, g).astype(jnp.float32) * heads_of(a_ref, s, g).astype(
                jnp.float32
            )
            delta = jnp.sum(product.T, axis=0, keepdims=True)
            found.append((pos, first, delta))
        return found

    def heads_of(ref, s, g):
        return jnp.concatenate(
            [
                ref[s, g * step : (g + 1) * step, h * head : (h + 1) * head]
                for h in range(heads)
            ],
            axis=0,
        )

    def dot(a, b, ca, cb):
        return lax.dot_general(
            a, b, (((ca,), (cb,)), ((), ())), preferred_element_type=jnp.float32
        )

    def attend(s, g, found):
        pos, first, delta = found
        low, high = max(g - 1, 0) * step, (g + 1) * step
        key_count = kpos.shape[1] * (high - low)
        key_block = kv[s, :, low:high, 0:head].reshape(key_count, head)
        value_block = kv[s, :, low:high, head : 2 * head].reshape(key_count, head)
        key_pos = kpos[s, :, low:high, :].reshape(key_count, LANES)
        query_n, grad_n = heads_of(q_ref, s, g), heads_of(g_ref, s, g)
        live = (key_pos <= pos) & (key_pos >= first)
        scores = jnp.where(live, dot(key_block, query_n, 1, 1) * scale, NEG_FILL)
        terms = jnp.exp(scores - jnp.max(scores, axis=0, keepdims=True))
        probs = terms * (1.0 / jnp.sum(terms, axis=0, keepdims=True))
        prob_grad = dot(value_block, grad_n, 1, 1)
        score_grad = (probs * (prob_grad - delta)).astype(jnp.bfloat16)
        value_grad = dot(probs.astype(jnp.bfloat16), grad_n, 1, 0)
        key_grad = dot(score_grad, query_n, 1, 0) * scale
        query_grad = dot(score_grad, key_block, 0, 0) * scale
        for h in range(heads):
            dq_ref[s, g * step : (g + 1) * step, h * head : (h + 1) * head] = query_grad[
                h * step : (h + 1) * step
            ].astype(dq_ref.dtype)
        span = high - low
        shape = (outer, INNER, span, head)
        for part, grad in ((0, key_grad), (1, value_grad)):
            grad = grad.reshape(shape)
            cols = slice(part * head, (part + 1) * head)
            if span > step:
                acc[s, :, :, low : low + step, cols] += grad[:, :, :step]
            acc[s, :, :, high - step : high, cols] = grad[:, :, span - step :]

    def plane_start(s):
        for k in range(1, INNER):
            plane_out[s, k - 1] = acc[s, :, inner_of(k)].astype(jnp.bfloat16)
            start(
                copy_to(
                    plane_out.at[s, k - 1],
                    plane_in.at[s, k - 1],
                    plane_send.at[s, k - 1],
                    plane_recv.at[s, k - 1],
                    ctx_of(o_me, inner_of(k)),
                    pair,
                )
            )

    def outer_start(s):
        total = acc[s, :, i_me]
        for k in range(1, INNER):
            copy_to(
                plane_out.at[s, k - 1],
                plane_in.at[s, k - 1],
                plane_send.at[s, k - 1],
                plane_recv.at[s, k - 1],
                me,
                pair,
            ).wait_recv()
            total += plane_in[s, k - 1].astype(jnp.float32)
        plane_sum[s] = total
        for m in range(1, outer):
            outer_out[s, m - 1] = plane_sum[s, outer_of(m)].astype(jnp.bfloat16)
            start(
                copy_to(
                    outer_out.at[s, m - 1],
                    outer_in.at[s, m - 1],
                    outer_send.at[s, m - 1],
                    outer_recv.at[s, m - 1],
                    ctx_of(outer_of(m), i_me),
                    pair,
                )
            )

    def kvg_start(s):
        total = plane_sum[s, o_me]
        for m in range(1, outer):
            copy_to(
                outer_out.at[s, m - 1],
                outer_in.at[s, m - 1],
                outer_send.at[s, m - 1],
                outer_recv.at[s, m - 1],
                me,
                pair,
            ).wait_recv()
            total += outer_in[s, m - 1].astype(jnp.float32)
        cut = slice(s * rows, (s + 1) * rows)
        kvg[0, cut] = total.astype(jnp.bfloat16)
        for n, (k, e) in enumerate(slots[1:], 1):
            start(
                copy_to(
                    kvg.at[0, cut],
                    kvg.at[n, cut],
                    kvg_send.at[s, n - 1],
                    kvg_recv.at[s, n - 1],
                    ctx_of(o_me, inner_of(k)),
                    (pair + e) % pairs,
                )
            )

    def x_source(o, i, d):
        if x_ref.ndim == 2:
            first = (ctx_of(o, i) * pairs + d) * width
            return x_ref.at[:, pl.ds(pl.multiple_of(first, LANES), width)]
        return x_ref.at[i * pairs + d]

    def x_target(n, o):
        return xg.at[n, o] if x_ref.ndim == 2 else xg.at[n]

    found = []
    for s in range(seqs):
        found.append(query_rows(s))
        forward(s)

    own_copies = []
    for o in range(x_parts):
        own_copies.append(
            pltpu.make_async_copy(x_source(o, i_me, pair), x_target(0, o), own_sem.at[o])
        )
        own_copies[-1].start()
    for n, (k, e) in enumerate(slots[1:], 1):
        for o in range(x_parts):
            start(
                copy_to(
                    x_source(o, inner_of(k), (pair + e) % pairs),
                    x_target(n, o),
                    x_send.at[n - 1, o],
                    x_recv.at[n - 1, o],
                    ctx_of(o_me, inner_of(k)),
                    (pair + e) % pairs,
                )
            )

    for s in range(seqs):
        for k in range(1, INNER):
            for o in range(outer):
                arrived(s, ctx_of(outer_of(o), inner_of(k)))
        for g in range(groups):
            attend(s, g, found[s][g])
        plane_start(s)
    for s in range(seqs):
        outer_start(s)
    for s in range(seqs):
        kvg_start(s)

    for copy in own_copies:
        copy.wait()
    for n, (k, e) in enumerate(slots[1:], 1):
        for o in range(x_parts):
            copy_to(
                x_source(o, i_me, pair),
                x_target(n, o),
                x_send.at[n - 1, o],
                x_recv.at[n - 1, o],
                me,
                pair,
            ).wait_recv()
    for s in range(seqs):
        cut = slice(s * rows, (s + 1) * rows)
        for n in range(1, len(slots)):
            copy_to(
                kvg.at[0, cut],
                kvg.at[n, cut],
                kvg_send.at[s, n - 1],
                kvg_recv.at[s, n - 1],
                me,
                pair,
            ).wait_recv()

    depth = len(slots) * seqs * rows
    kv_grads = kvg[...].reshape(depth, 2 * head)
    for o in range(outer):
        wsum[o] = dot(xg[:, o].reshape(depth, xg.shape[3]), kv_grads, 0, 0)
    for m in range(1, outer):
        w_out[m - 1] = wsum[outer_of(m)].astype(jnp.bfloat16)
        start(
            copy_to(
                w_out.at[m - 1],
                w_in.at[m - 1],
                w_send.at[m - 1],
                w_recv.at[m - 1],
                ctx_of(outer_of(m), i_me),
                pair,
            )
        )
    total = wsum[o_me]
    for m in range(1, outer):
        copy_to(
            w_out.at[m - 1], w_in.at[m - 1], w_send.at[m - 1], w_recv.at[m - 1], me, pair
        ).wait_recv()
        total += w_in[m - 1].astype(jnp.float32)
    w_fin[pair] = total[:width]
    for e in range(1, pairs):
        start(
            copy_to(
                w_fin.at[pair],
                w_fin.at[pair],
                fin_send.at[e - 1],
                fin_recv.at[e - 1],
                me,
                (pair + e) % pairs,
            )
        )
    for e in range(1, pairs):
        src = (pair + pairs - e) % pairs
        copy_to(
            w_fin.at[src], w_fin.at[src], fin_send.at[e - 1], fin_recv.at[e - 1], me, pair
        ).wait_recv()
    dw_ref[...] = w_fin[...].reshape(dw_ref.shape)
    for copy in pending:
        copy.wait_send()


def local(
    layer_input, queries, key_states, value_states, attn_output, out_grad, doc_ids, positions
):
    seqs, rows, model = layer_input.shape
    head = key_states.shape[2]
    ctx = lax.axis_size("ctx")
    pairs = lax.axis_size("dp")
    outer = ctx // INNER
    width = model // (ctx * pairs)
    padded = -(-width // LANES) * LANES
    slots = INNER * pairs
    flat_rows = seqs * rows
    flat = layer_input.reshape(flat_rows, model)
    if padded == width:
        x_parts = outer
    else:
        x_parts = 1
        flat = flat.reshape(flat_rows, outer, INNER * pairs, width).transpose(2, 1, 0, 3)
        flat = jnp.pad(flat, ((0, 0), (0, 0), (0, 0), (0, padded - width)))
    vmem = pl.BlockSpec(memory_space=pltpu.VMEM)
    both = 2 * head
    sends = (outer - 1) + (INNER - 1) + (INNER - 1) * (outer - 1)
    dma = pltpu.SemaphoreType.DMA
    f32, bf16 = jnp.float32, jnp.bfloat16
    return pl.pallas_call(
        functools.partial(kernel, (outer, pairs, width)),
        out_shape=(
            jax.ShapeDtypeStruct(queries.shape, bf16),
            jax.ShapeDtypeStruct((model // ctx, both), f32),
        ),
        in_specs=[pl.BlockSpec(memory_space=pl.ANY)] + [vmem] * 7,
        out_specs=(vmem, vmem),
        scratch_shapes=[
            pltpu.VMEM((seqs, ctx, rows, both), bf16),
            pltpu.VMEM((seqs, ctx, rows, LANES), f32),
            pltpu.VMEM((seqs, ctx * rows, LANES), f32),
            pltpu.VMEM((seqs, outer, INNER, rows, both), f32),
            pltpu.VMEM((seqs, INNER - 1, outer, rows, both), bf16),
            pltpu.VMEM((seqs, INNER - 1, outer, rows, both), bf16),
            pltpu.VMEM((seqs, outer, rows, both), f32),
            pltpu.VMEM((seqs, outer - 1, rows, both), bf16),
            pltpu.VMEM((seqs, outer - 1, rows, both), bf16),
            pltpu.VMEM((slots, flat_rows, both), bf16),
            pltpu.VMEM((slots, outer, flat_rows, padded), bf16),
            pltpu.VMEM((outer, padded, both), f32),
            pltpu.VMEM((outer - 1, padded, both), bf16),
            pltpu.VMEM((outer - 1, padded, both), bf16),
            pltpu.VMEM((pairs, width, both), f32),
            dma((seqs, sends)),
            dma((seqs, ctx)),
            dma((seqs, INNER - 1)),
            dma((seqs, INNER - 1)),
            dma((seqs, outer - 1)),
            dma((seqs, outer - 1)),
            dma((seqs, slots - 1)),
            dma((seqs, slots - 1)),
            dma((slots - 1, x_parts)),
            dma((slots - 1, x_parts)),
            dma((outer - 1,)),
            dma((outer - 1,)),
            dma((pairs - 1,)),
            dma((pairs - 1,)),
            dma((x_parts,)),
        ],
        compiler_params=pltpu.CompilerParams(
            collective_id=0, has_side_effects=True, vmem_limit_bytes=60 * 1024 * 1024
        ),
    )(flat, queries, key_states, value_states, attn_output, out_grad, doc_ids, positions)


def solution(mesh):
    in_specs = (
        P("dp", "ctx", None),
        P("dp", "ctx", None),
        P("dp", "ctx", None),
        P("dp", "ctx", None),
        P("dp", "ctx", None),
        P("dp", "ctx", None),
        P("dp", None),
        P("dp", None),
    )
    out_specs = (P("dp", "ctx", None), P("ctx", None))
    return jax.shard_map(local, mesh=mesh, in_specs=in_specs, out_specs=out_specs, check_vma=False)
```

time: 400 us -> 66.3 us (0.17)
  waiting for transfers between devices: 200 us -> 0 us
  blocking collectives: 88.6 us -> 0 us
  Pallas kernels: 0 us -> 63.1 us
  matrix products: 61.9 us -> 0 us
  local copies, waits for them, and re-layouts: 23.4 us -> 2.42 us
  between operations: 14.5 us -> 0.65 us
    ppermute x15 -> x0, waiting for transfers between devices: 94.2 us -> none  [passed_along(): lax.ppermute(x, axis, [(i, (i + by) % length) for i in range(length)])]
    reduce_scatter x1 -> x0, waiting for transfers between devices: 89 us -> none  [local(): lax.psum_scatter(lax.dot_general(flat_input, flat_grad, (((0,), (0,)), ((...]
    all_gather x2 -> x0, blocking collectives: 88.6 us -> none  [the longest x1 47.9 us: local(): lax.all_gather(key_states, 'ctx', axis=1, tiled=True)]
    pallas_call x0 -> x1, Pallas kernels: none -> 63.1 us  [local(): pl.pallas_call(functools.partial(kernel, (outer, pairs, width)), out_shap...]
    dot_general x85 -> x0, matrix products: 61.9 us -> none  [the longest x20 21.1 us: scores_of(): jnp.einsum('skd,snd->skn', key_block, query_n, preferred_element_type=jnp...]
    gather x2 -> x0, local copies, waits for them, and re-layouts: 17.7 us -> none  [local(): doc_full = jnp.take_along_axis(doc_ids, positions, axis=1)]
    psum x1 -> x0, waiting for transfers between devices: 17.3 us -> none  [local(): weight_grad = lax.psum(row_share, 'dp')]
  transfers between devices with their start and end apart: 17 -> 0, of which waited for: 14 -> 0; matrix products, arithmetic and copies ran while one was open for 11% -> 0% of each run, Pallas kernels for 0% -> 0%
where the time goes in v1:
time: 66.3 us; the launch traced here: 66.1 us
  Pallas kernels  63.1 us (95%)
  local copies, waits for them, and re-layouts  2.42 us (4%)
    pallas_call x1, Pallas kernels, local(): pl.pallas_call(functools.partial(kernel, (outer, pairs, width)), out_shap...  63.1 us
    unnamed x4, local copies, waits for them, and re-layouts  2.42 us

profile of v1, /device:TPU:0, one launch (start us, length us, event | category | flops | bytes accessed | tf_op | source)
XLA Modules:
  0.0 66.1 jit_solution(10001100950825101767)
XLA Ops:
  0.6 63.1 %shard_map.95 = (bf16[2,64,1024]{2,1,0:T(8,128)(2,1)}, f32[256,256]{1,0:T(8,128)}) custom-call(bf16[128,4096]{1,0:T(8,128)(2,1)} %bitcast.1, bf16[2,64,1024]{2,1,0:T(8,128)(2,1)} %q_ref.1, bf16[2,64,128]{2,1,0:T(8,128)(2,1)} %k_ref.1, bf16[2,64,128]{2,1,0:T(8,128)(2,1)} %v_ref.1, bf16[2,64,1024]{2,1,0:T(8,128)(2,1)} %a_ref.1, bf16[2,64,1024]{2,1,0:T(8,128)(2,1)} %g_ref.1, ...), custom_call_target="tpu_custom_call" | custom-call | tf_op jit(solution)/shard_map/pallas_call | solution.py:445
  63.7 0.0 copy-start
  63.7 1.7 %copy.12 = bf16[2,64,1024]{2,1,0:T(8,128)(2,1)} copy(bf16[2,64,1024]{2,1,0:T(8,128)(2,1)} %get-tuple-element.4) | data formatting | bytes 524288
  65.4 0.0 copy-done
  65.4 0.7 %copy.13 = f32[256,256]{1,0:T(8,128)} copy(f32[256,256]{1,0:T(8,128)S(1)} %copy-done) | data formatting | bytes 524288
Async XLA Ops:
  63.7 1.7 %copy-start = (f32[256,256]{1,0:T(8,128)S(1)}, f32[256,256]{1,0:T(8,128)}, u32[]{:S(2)}) copy-start(f32[256,256]{1,0:T(8,128)} %get-tuple-element.5) | copy-start | bytes 786436

commit v2 on v0

v2 whole, which is shorter than its diff:
```python
import functools
import math

import jax
import jax.numpy as jnp
from jax import lax
from jax.experimental import pallas as pl
from jax.experimental.pallas import tpu as pltpu
from jax.sharding import PartitionSpec as P

NEG_FILL = -1e30
INNER = 4
LANES = 128


GROUPS = 4
HALVES = 2


def kernel(
    dims,
    x_ref,
    q_ref,
    k_ref,
    v_ref,
    a_ref,
    g_ref,
    doc_ref,
    pos_ref,
    dq_ref,
    dw_ref,
    kv,
    kv_swap,
    q_in,
    g_in,
    delta_own,
    delta_out,
    delta_in,
    dq_out,
    dq_in,
    kpos,
    dcol,
    acc,
    y_out,
    y_in,
    y_sum,
    z_out,
    z_in,
    z_sum,
    kvg,
    xg,
    wsum,
    w_out,
    w_in,
    w_fin,
    send_sem,
    swap_recv,
    ag_recv,
    y_recv,
    z_recv,
    kvg_recv,
    x_recv,
    w_recv,
    fin_recv,
    own_sem,
):
    outer, pairs, width = dims
    seqs, rows, head = k_ref.shape
    heads = q_ref.shape[2] // head
    step = rows // GROUPS
    scale = 1.0 / math.sqrt(head)
    x_parts = outer if x_ref.ndim == 2 else 1
    ctx_count = outer * INNER

    me = lax.axis_index("ctx")
    pair = lax.axis_index("dp")
    o_me, i_me = me // INNER, me % INNER
    col, row = i_me % 2, i_me // 2
    other = (col + 1) % 2

    def inner_of(k):
        return ((row + k // 2) % 2) * 2 + (col + k % 2) % 2

    def outer_of(m):
        return (o_me + m) % outer

    def ctx_of(o, i):
        return o * INNER + i

    side, across = ctx_of(o_me, inner_of(1)), ctx_of(o_me, inner_of(2))

    pending = []

    def copy_to(src, dst, recv_sem, ctx, dp, slot):
        return pltpu.make_async_remote_copy(
            src_ref=src,
            dst_ref=dst,
            send_sem=send_sem.at[slot],
            recv_sem=recv_sem,
            device_id={"ctx": ctx, "dp": dp},
            device_id_type=pl.DeviceIdType.MESH,
        )

    def send(src, dst, recv_sem, ctx, dp):
        copy = copy_to(src, dst, recv_sem, ctx, dp, len(pending))
        copy.start()
        pending.append(copy)

    def landed(dst, recv_sem):
        copy_to(dst, dst, recv_sem, side, pair, 0).wait_recv()

    slots = [(k, e) for k in range(INNER) for e in range(pairs)]

    barrier = pltpu.get_barrier_semaphore()
    greeted = [(ctx_of(outer_of(m), i_me), pair) for m in range(1, outer)]
    greeted += [(ctx_of(o_me, inner_of(k)), (pair + e) % pairs) for k, e in slots[1:]]
    for ctx, dp in greeted:
        pl.semaphore_signal(
            barrier,
            inc=1,
            device_id={"ctx": ctx, "dp": dp},
            device_id_type=pl.DeviceIdType.MESH,
        )

    def heads_of(block):
        return jnp.concatenate(
            [block[:, h * head : (h + 1) * head] for h in range(heads)], axis=0
        )

    def delta_rows(s, g):
        cut = slice(g * step, (g + 1) * step)
        product = heads_of(g_ref[s, cut, :].astype(jnp.float32)) * heads_of(
            a_ref[s, cut, :].astype(jnp.float32)
        )
        return jnp.sum(product.T, axis=0, keepdims=True)

    kv[me, :, 0:head] = k_ref[col]
    kv[me, :, head : 2 * head] = v_ref[col]
    kv_swap[:, 0:head] = k_ref[other]
    kv_swap[:, head : 2 * head] = v_ref[other]
    pl.semaphore_wait(barrier, len(greeted))

    def half(h):
        return pl.ds(h * (rows // HALVES), rows // HALVES)

    def block_send(src, h, ctx):
        send(kv.at[src, half(h)], kv.at[src, half(h)], ag_recv.at[h, src], ctx, pair)

    def block_landed(src, h):
        landed(kv.at[src, half(h)], ag_recv.at[h, src])

    for h in range(HALVES):
        send(kv_swap.at[half(h)], kv.at[me, half(h)], ag_recv.at[h, me], side, pair)
        for m in range(1, outer):
            block_send(me, h, ctx_of(outer_of(m), i_me))
        block_send(me, h, across)
    send(q_ref.at[other], q_in, swap_recv.at[0], side, pair)
    send(g_ref.at[other], g_in, swap_recv.at[1], side, pair)
    for h in range(HALVES):
        block_landed(side, h)
        for m in range(1, outer):
            block_send(side, h, ctx_of(outer_of(m), i_me))
        block_send(side, h, across)

    for g in range(GROUPS):
        delta_out[g : g + 1, :] = delta_rows(other, g)
    send(delta_out, delta_in, swap_recv.at[2], side, pair)
    for g in range(GROUPS):
        delta_own[g : g + 1, :] = delta_rows(col, g)

    def columns_of(line):
        return jnp.broadcast_to(line, (LANES, LANES)).T

    total_rows = ctx_count * rows
    per = LANES // rows
    pos_line = pos_ref[pl.ds(col, 1), :].astype(jnp.float32)
    doc_line = doc_ref[pl.ds(col, 1), :].astype(jnp.float32)
    for b in range(total_rows // LANES):
        cut = slice(b * LANES, (b + 1) * LANES)
        kpos[b * per : (b + 1) * per] = columns_of(pos_line[:, cut]).reshape(per, rows, LANES)
        dcol[cut] = columns_of(doc_line[:, cut])

    def forward(h):
        for m in range(1, outer):
            o = outer_of(outer - m)
            for src in (ctx_of(o, i_me), ctx_of(o, inner_of(1))):
                block_landed(src, h)
                block_send(src, h, across)

    forward(0)

    place = lax.broadcasted_iota(jnp.int32, (total_rows, LANES), 0).astype(jnp.float32)
    sub = lax.broadcasted_iota(jnp.int32, (step, LANES), 0)
    lane = lax.broadcasted_iota(jnp.int32, (step, LANES), 1)
    pick = sub == lane % step
    doc_cols = dcol[...]

    def query_row(g, src):
        own = kpos[src, g * step : (g + 1) * step, :]
        pos = jnp.sum(jnp.where(pick, own, 0.0), axis=0, keepdims=True)
        doc = jnp.sum(jnp.where(place == pos, doc_cols, 0.0), axis=0, keepdims=True)
        first = jnp.sum(jnp.where(doc_cols < doc, 1.0, 0.0), axis=0, keepdims=True)
        return pos, first

    found = []
    for g in range(GROUPS):
        own_row, side_row = query_row(g, me), query_row(g, side)
        found.append(
            tuple(jnp.concatenate([a, b], axis=1) for a, b in zip(own_row, side_row))
        )
    forward(1)

    def x_source(o, i, d):
        if x_ref.ndim == 2:
            first = (ctx_of(o, i) * pairs + d) * width
            return x_ref.at[:, pl.ds(pl.multiple_of(first, LANES), width)]
        return x_ref.at[i * pairs + d]

    def x_target(n, o):
        return xg.at[n, o] if x_ref.ndim == 2 else xg.at[n]

    own_copies = []
    for o in range(x_parts):
        own_copies.append(
            pltpu.make_async_copy(x_source(o, i_me, pair), x_target(0, o), own_sem.at[o])
        )
        own_copies[-1].start()

    def x_start(chosen):
        for n, (k, e) in enumerate(slots):
            if n and k == chosen:
                for o in range(x_parts):
                    send(
                        x_source(o, inner_of(k), (pair + e) % pairs),
                        x_target(n, o),
                        x_recv.at[n - 1, o],
                        ctx_of(o_me, inner_of(k)),
                        (pair + e) % pairs,
                    )

    def dot(a, b, ca, cb):
        return lax.dot_general(
            a, b, (((ca,), (cb,)), ((), ())), preferred_element_type=jnp.float32
        )

    def attend(g):
        pos, first = found[g]
        low, high = max(g - 1, 0) * step, (g + 1) * step
        span = high - low
        key_count = ctx_count * span
        cut = slice(g * step, (g + 1) * step)
        key_block = kv[:, low:high, 0:head].reshape(key_count, head)
        value_block = kv[:, low:high, head : 2 * head].reshape(key_count, head)
        key_pos = kpos[:, low:high, :].reshape(key_count, LANES)
        key_pos = jnp.concatenate([key_pos, key_pos], axis=1)
        query_n = jnp.concatenate(
            [heads_of(q_ref[col, cut, :]), heads_of(q_in[cut, :])], axis=0
        )
        grad_n = jnp.concatenate(
            [heads_of(g_ref[col, cut, :]), heads_of(g_in[cut, :])], axis=0
        )
        delta = jnp.concatenate([delta_own[g : g + 1, :], delta_in[g : g + 1, :]], axis=1)
        live = (key_pos <= pos) & (key_pos >= first)
        scores = jnp.where(live, dot(key_block, query_n, 1, 1) * scale, NEG_FILL)
        terms = jnp.exp(scores - jnp.max(scores, axis=0, keepdims=True))
        probs = terms * (1.0 / jnp.sum(terms, axis=0, keepdims=True))
        prob_grad = dot(value_block, grad_n, 1, 1)
        score_grad = (probs * (prob_grad - delta)).astype(jnp.bfloat16)
        value_grad = dot(probs.astype(jnp.bfloat16), grad_n, 1, 0)
        key_grad = dot(score_grad, query_n, 1, 0) * scale
        query_grad = (dot(score_grad, key_block, 0, 0) * scale).astype(jnp.bfloat16)
        for h in range(heads):
            cols = slice(h * head, (h + 1) * head)
            dq_ref[col, cut, cols] = query_grad[h * step : (h + 1) * step]
            dq_out[cut, cols] = query_grad[(heads + h) * step : (heads + h + 1) * step]
        for part, grad in ((0, key_grad), (1, value_grad)):
            grad = grad.reshape(outer, 2, 2, span, head)
            cols = slice(part * head, (part + 1) * head)
            if span > step:
                acc[g - 1, :, :, :, :, cols] += grad[:, :, :, :step]
            acc[g, :, :, :, :, cols] = grad[:, :, :, span - step :]

    def y_start(b):
        y_out[b] = acc[b, :, (row + 1) % 2].astype(jnp.bfloat16)
        send(y_out.at[b], y_in.at[b], y_recv.at[b], across, pair)

    def z_start(b):
        landed(y_in.at[b], y_recv.at[b])
        y_sum[b] = acc[b, :, row] + y_in[b].astype(jnp.float32)
        for m in range(1, outer):
            z_out[b, m - 1] = y_sum[b, outer_of(m)].astype(jnp.bfloat16)
            send(
                z_out.at[b, m - 1],
                z_in.at[b, m - 1],
                z_recv.at[b, m - 1],
                ctx_of(outer_of(m), i_me),
                pair,
            )

    def z_finish(b):
        total = y_sum[b, o_me]
        for m in range(1, outer):
            landed(z_in.at[b, m - 1], z_recv.at[b, m - 1])
            total += z_in[b, m - 1].astype(jnp.float32)
        z_sum[:, b * step : (b + 1) * step, :] = total.astype(jnp.bfloat16)

    def wait_half(h):
        for o in range(outer):
            for k in (2, 3):
                block_landed(ctx_of(outer_of(o), inner_of(k)), h)

    x_start(0)
    wait_half(0)
    landed(q_in, swap_recv.at[0])
    landed(g_in, swap_recv.at[1])
    landed(delta_in, swap_recv.at[2])
    x_start(1)
    for g in range(GROUPS):
        if g == GROUPS // HALVES:
            wait_half(1)
            x_start(2)
        attend(g)
        if g >= 1:
            y_start(g - 1)
        if g >= 2:
            z_start(g - 2)
    y_start(GROUPS - 1)
    send(dq_out, dq_in, swap_recv.at[3], side, pair)
    z_start(GROUPS - 2)
    z_start(GROUPS - 1)
    x_start(3)
    for b in range(GROUPS):
        z_finish(b)

    def kvg_at(k, e, s):
        return kvg.at[k * pairs + e, s], kvg_recv.at[k * pairs + e, s]

    def pass_on(k, s):
        for e in range(1, pairs):
            dst, recv_sem = kvg_at(k, e, s)
            send(kvg_at(k, 0, s)[0], dst, recv_sem, me, (pair + e) % pairs)

    for k in range(1, INNER):
        for b in range(2):
            dst, recv_sem = kvg_at(k // 2 * 2 + b, 0, col)
            send(
                z_sum.at[(col + k + b) % 2],
                dst,
                recv_sem,
                ctx_of(o_me, inner_of(k)),
                pair,
            )
    for b in range(2):
        kvg[b * pairs, col] = z_sum[(col + b) % 2]
        pass_on(b, col)
    for b in range(2):
        landed(*kvg_at(b, 0, other))
        pass_on(b, other)
    for b in (2, 3):
        for s in range(seqs):
            landed(*kvg_at(b, 0, s))
            pass_on(b, s)

    landed(dq_in, swap_recv.at[3])
    dq_ref[other] = dq_in[...]
    for copy in own_copies:
        copy.wait()
    for n in range(1, len(slots)):
        for o in range(x_parts):
            landed(x_target(n, o), x_recv.at[n - 1, o])
    for k in range(INNER):
        for e in range(1, pairs):
            for s in range(seqs):
                landed(*kvg_at(k, e, s))

    depth = len(slots) * seqs * rows
    kv_grads = kvg[...].reshape(depth, 2 * head)
    for o in range(outer):
        wsum[o] = dot(xg[:, o].reshape(depth, xg.shape[3]), kv_grads, 0, 0)
    for m in range(1, outer):
        w_out[m - 1] = wsum[outer_of(m)].astype(jnp.bfloat16)
        send(
            w_out.at[m - 1], w_in.at[m - 1], w_recv.at[m - 1], ctx_of(outer_of(m), i_me), pair
        )
    total = wsum[o_me]
    for m in range(1, outer):
        landed(w_in.at[m - 1], w_recv.at[m - 1])
        total += w_in[m - 1].astype(jnp.float32)
    w_fin[pair] = total[:width]
    for e in range(1, pairs):
        send(w_fin.at[pair], w_fin.at[pair], fin_recv.at[e - 1], me, (pair + e) % pairs)
    for e in range(1, pairs):
        landed(w_fin.at[(pair + pairs - e) % pairs], fin_recv.at[e - 1])
    dw_ref[...] = w_fin[...].reshape(dw_ref.shape)
    for copy in pending:
        copy.wait_send()


def local(
    layer_input, queries, key_states, value_states, attn_output, out_grad, doc_ids, positions
):
    seqs, rows, model = layer_input.shape
    head = key_states.shape[2]
    ctx = lax.axis_size("ctx")
    pairs = lax.axis_size("dp")
    outer = ctx // INNER
    width = model // (ctx * pairs)
    padded = -(-width // LANES) * LANES
    slots = INNER * pairs
    flat_rows = seqs * rows
    flat = layer_input.reshape(flat_rows, model)
    if padded == width:
        x_parts = outer
    else:
        x_parts = 1
        flat = flat.reshape(flat_rows, outer, INNER * pairs, width).transpose(2, 1, 0, 3)
        flat = jnp.pad(flat, ((0, 0), (0, 0), (0, 0), (0, padded - width)))
    vmem = pl.BlockSpec(memory_space=pltpu.VMEM)
    both = 2 * head
    sends = HALVES * (4 * outer + 1) + 4 + GROUPS * outer + 6 + 8 * (pairs - 1)
    sends += (slots - 1) * x_parts + (outer - 1) + (pairs - 1)
    dma = pltpu.SemaphoreType.DMA
    f32, bf16 = jnp.float32, jnp.bfloat16
    step = rows // GROUPS
    query_width = queries.shape[2]
    return pl.pallas_call(
        functools.partial(kernel, (outer, pairs, width)),
        out_shape=(
            jax.ShapeDtypeStruct(queries.shape, bf16),
            jax.ShapeDtypeStruct((model // ctx, both), f32),
        ),
        in_specs=[pl.BlockSpec(memory_space=pl.ANY)] + [vmem] * 7,
        out_specs=(vmem, vmem),
        scratch_shapes=[
            pltpu.VMEM((ctx, rows, both), bf16),
            pltpu.VMEM((rows, both), bf16),
            pltpu.VMEM((rows, query_width), bf16),
            pltpu.VMEM((rows, query_width), bf16),
            pltpu.VMEM((8, LANES), f32),
            pltpu.VMEM((8, LANES), f32),
            pltpu.VMEM((8, LANES), f32),
            pltpu.VMEM((rows, query_width), bf16),
            pltpu.VMEM((rows, query_width), bf16),
            pltpu.VMEM((ctx, rows, LANES), f32),
            pltpu.VMEM((ctx * rows, LANES), f32),
            pltpu.VMEM((GROUPS, outer, 2, 2, step, both), f32),
            pltpu.VMEM((GROUPS, outer, 2, step, both), bf16),
            pltpu.VMEM((GROUPS, outer, 2, step, both), bf16),
            pltpu.VMEM((GROUPS, outer, 2, step, both), f32),
            pltpu.VMEM((GROUPS, outer - 1, 2, step, both), bf16),
            pltpu.VMEM((GROUPS, outer - 1, 2, step, both), bf16),
            pltpu.VMEM((2, rows, both), bf16),
            pltpu.VMEM((slots, seqs, rows, both), bf16),
            pltpu.VMEM((slots, outer, flat_rows, padded), bf16),
            pltpu.VMEM((outer, padded, both), f32),
            pltpu.VMEM((outer - 1, padded, both), bf16),
            pltpu.VMEM((outer - 1, padded, both), bf16),
            pltpu.VMEM((pairs, width, both), f32),
            dma((sends,)),
            dma((4,)),
            dma((HALVES, ctx)),
            dma((GROUPS,)),
            dma((GROUPS, outer - 1)),
            dma((slots, seqs)),
            dma((slots - 1, x_parts)),
            dma((outer - 1,)),
            dma((pairs - 1,)),
            dma((x_parts,)),
        ],
        compiler_params=pltpu.CompilerParams(
            collective_id=0, has_side_effects=True, vmem_limit_bytes=60 * 1024 * 1024
        ),
    )(flat, queries, key_states, value_states, attn_output, out_grad, doc_ids, positions)


def solution(mesh):
    in_specs = (
        P("dp", "ctx", None),
        P("dp", "ctx", None),
        P("dp", "ctx", None),
        P("dp", "ctx", None),
        P("dp", "ctx", None),
        P("dp", "ctx", None),
        P("dp", None),
        P("dp", None),
    )
    out_specs = (P("dp", "ctx", None), P("ctx", None))
    return jax.shard_map(local, mesh=mesh, in_specs=in_specs, out_specs=out_specs, check_vma=False)
```

time: 400 us -> 55.1 us (0.14)
  waiting for transfers between devices: 200 us -> 0 us
  blocking collectives: 88.6 us -> 0 us
  matrix products: 61.9 us -> 0 us
  Pallas kernels: 0 us -> 51.8 us
  local copies, waits for them, and re-layouts: 23.4 us -> 2.42 us
  between operations: 14.5 us -> 0.65 us
    ppermute x15 -> x0, waiting for transfers between devices: 94.2 us -> none  [passed_along(): lax.ppermute(x, axis, [(i, (i + by) % length) for i in range(length)])]
    reduce_scatter x1 -> x0, waiting for transfers between devices: 89 us -> none  [local(): lax.psum_scatter(lax.dot_general(flat_input, flat_grad, (((0,), (0,)), ((...]
    all_gather x2 -> x0, blocking collectives: 88.6 us -> none  [the longest x1 47.9 us: local(): lax.all_gather(key_states, 'ctx', axis=1, tiled=True)]
    dot_general x85 -> x0, matrix products: 61.9 us -> none  [the longest x20 21.1 us: scores_of(): jnp.einsum('skd,snd->skn', key_block, query_n, preferred_element_type=jnp...]
    pallas_call x0 -> x1, Pallas kernels: none -> 51.8 us  [local(): pl.pallas_call(functools.partial(kernel, (outer, pairs, width)), out_shap...]
    gather x2 -> x0, local copies, waits for them, and re-layouts: 17.7 us -> none  [local(): doc_full = jnp.take_along_axis(doc_ids, positions, axis=1)]
    psum x1 -> x0, waiting for transfers between devices: 17.3 us -> none  [local(): weight_grad = lax.psum(row_share, 'dp')]
  transfers between devices with their start and end apart: 17 -> 0, of which waited for: 14 -> 0; matrix products, arithmetic and copies ran while one was open for 11% -> 0% of each run, Pallas kernels for 0% -> 0%
where the time goes in v2:
time: 55.1 us; the launch traced here: 54.9 us
  Pallas kernels  51.8 us (94%)
  local copies, waits for them, and re-layouts  2.42 us (4%)
  between operations  0.65 us (1%)
    pallas_call x1, Pallas kernels, local(): pl.pallas_call(functools.partial(kernel, (outer, pairs, width)), out_shap...  51.8 us
    unnamed x4, local copies, waits for them, and re-layouts  2.42 us

profile of v2, /device:TPU:0, one launch (start us, length us, event | category | flops | bytes accessed | tf_op | source)
XLA Modules:
  0.0 54.9 jit_solution(491966382522472770)
XLA Ops:
  0.6 51.8 %shard_map.95 = (bf16[2,64,1024]{2,1,0:T(8,128)(2,1)}, f32[256,256]{1,0:T(8,128)}) custom-call(bf16[128,4096]{1,0:T(8,128)(2,1)} %bitcast.1, bf16[2,64,1024]{2,1,0:T(8,128)(2,1)} %q_ref.1, bf16[2,64,128]{2,1,0:T(8,128)(2,1)} %k_ref.1, bf16[2,64,128]{2,1,0:T(8,128)(2,1)} %v_ref.1, bf16[2,64,1024]{2,1,0:T(8,128)(2,1)} %a_ref.1, bf16[2,64,1024]{2,1,0:T(8,128)(2,1)} %g_ref.1, ...), custom_call_target="tpu_custom_call" | custom-call | tf_op jit(solution)/shard_map/pallas_call | solution.py:426
  52.5 0.0 copy-start
  52.5 1.7 %copy.12 = bf16[2,64,1024]{2,1,0:T(8,128)(2,1)} copy(bf16[2,64,1024]{2,1,0:T(8,128)(2,1)} %get-tuple-element.4) | data formatting | bytes 524288
  54.2 0.0 copy-done
  54.2 0.7 %copy.13 = f32[256,256]{1,0:T(8,128)} copy(f32[256,256]{1,0:T(8,128)S(1)} %copy-done) | data formatting | bytes 524288
Async XLA Ops:
  52.5 1.7 %copy-start = (f32[256,256]{1,0:T(8,128)S(1)}, f32[256,256]{1,0:T(8,128)}, u32[]{:S(2)}) copy-start(f32[256,256]{1,0:T(8,128)} %get-tuple-element.5) | copy-start | bytes 786436

commit v3 on v2

--- a/solution.py
+++ b/solution.py
@@ -49,12 +49,14 @@
     z_sum,
     kvg,
     xg,
+    xt,
     wsum,
     w_out,
     w_in,
     w_fin,
     send_sem,
     swap_recv,
+    side_recv,
     ag_recv,
     y_recv,
     z_recv,
@@ -154,8 +156,39 @@
         for m in range(1, outer):
             block_send(me, h, ctx_of(outer_of(m), i_me))
         block_send(me, h, across)
-    send(q_ref.at[other], q_in, swap_recv.at[0], side, pair)
-    send(g_ref.at[other], g_in, swap_recv.at[1], side, pair)
+    for g in range(GROUPS):
+        cut = pl.ds(g * step, step)
+        send(q_ref.at[other, cut], q_in.at[cut], swap_recv.at[g, 0], side, pair)
+        send(g_ref.at[other, cut], g_in.at[cut], swap_recv.at[g, 1], side, pair)
+    def x_source(o, i, d):
+        if x_ref.ndim == 2:
+            first = (ctx_of(o, i) * pairs + d) * width
+            return x_ref.at[:, pl.ds(pl.multiple_of(first, LANES), width)]
+        return x_ref.at[i * pairs + d]
+
+    def x_target(n, o):
+        return xg.at[n, o] if x_ref.ndim == 2 else xg.at[n]
+
+    own_copies = []
+    for o in range(x_parts):
+        own_copies.append(
+            pltpu.make_async_copy(x_source(o, i_me, pair), x_target(0, o), own_sem.at[o])
+        )
+        own_copies[-1].start()
+
+    def x_start(chosen, first=0, last=x_parts):
+        for n, (k, e) in enumerate(slots):
+            if n and k == chosen:
+                for o in range(first, last):
+                    send(
+                        x_source(o, inner_of(k), (pair + e) % pairs),
+                        x_target(n, o),
+                        x_recv.at[n - 1, o],
+                        ctx_of(o_me, inner_of(k)),
+                        (pair + e) % pairs,
+                    )
+
+    x_start(0)
     for h in range(HALVES):
         block_landed(side, h)
         for m in range(1, outer):
@@ -164,7 +197,15 @@
 
     for g in range(GROUPS):
         delta_out[g : g + 1, :] = delta_rows(other, g)
-    send(delta_out, delta_in, swap_recv.at[2], side, pair)
+    send(delta_out, delta_in, side_recv.at[0], side, pair)
+    def forward(h):
+        for m in range(1, outer):
+            o = outer_of(outer - m)
+            for src in (ctx_of(o, i_me), ctx_of(o, inner_of(1))):
+                block_landed(src, h)
+                block_send(src, h, across)
+
+    forward(0)
     for g in range(GROUPS):
         delta_own[g : g + 1, :] = delta_rows(col, g)
 
@@ -180,15 +221,7 @@
         kpos[b * per : (b + 1) * per] = columns_of(pos_line[:, cut]).reshape(per, rows, LANES)
         dcol[cut] = columns_of(doc_line[:, cut])
 
-    def forward(h):
-        for m in range(1, outer):
-            o = outer_of(outer - m)
-            for src in (ctx_of(o, i_me), ctx_of(o, inner_of(1))):
-                block_landed(src, h)
-                block_send(src, h, across)
-
-    forward(0)
-
+    forward(1)
     place = lax.broadcasted_iota(jnp.int32, (total_rows, LANES), 0).astype(jnp.float32)
     sub = lax.broadcasted_iota(jnp.int32, (step, LANES), 0)
     lane = lax.broadcasted_iota(jnp.int32, (step, LANES), 1)
@@ -208,35 +241,6 @@
         found.append(
             tuple(jnp.concatenate([a, b], axis=1) for a, b in zip(own_row, side_row))
         )
-    forward(1)
-
-    def x_source(o, i, d):
-        if x_ref.ndim == 2:
-            first = (ctx_of(o, i) * pairs + d) * width
-            return x_ref.at[:, pl.ds(pl.multiple_of(first, LANES), width)]
-        return x_ref.at[i * pairs + d]
-
-    def x_target(n, o):
-        return xg.at[n, o] if x_ref.ndim == 2 else xg.at[n]
-
-    own_copies = []
-    for o in range(x_parts):
-        own_copies.append(
-            pltpu.make_async_copy(x_source(o, i_me, pair), x_target(0, o), own_sem.at[o])
-        )
-        own_copies[-1].start()
-
-    def x_start(chosen):
-        for n, (k, e) in enumerate(slots):
-            if n and k == chosen:
-                for o in range(x_parts):
-                    send(
-                        x_source(o, inner_of(k), (pair + e) % pairs),
-                        x_target(n, o),
-                        x_recv.at[n - 1, o],
-                        ctx_of(o_me, inner_of(k)),
-                        (pair + e) % pairs,
-                    )
 
     def dot(a, b, ca, cb):
         return lax.dot_general(
@@ -309,80 +313,101 @@
             for k in (2, 3):
                 block_landed(ctx_of(outer_of(o), inner_of(k)), h)
 
-    x_start(0)
+    def kvg_at(k, e, s, h):
+        slot = k * pairs + e
+        return kvg.at[slot, s, half(h)], kvg_recv.at[h, slot, s]
+
+    def pass_on(k, s, h):
+        for e in range(1, pairs):
+            dst, recv_sem = kvg_at(k, e, s, h)
+            send(kvg_at(k, 0, s, h)[0], dst, recv_sem, me, (pair + e) % pairs)
+
+    def kvg_start(h):
+        for k in range(1, INNER):
+            for b in range(2):
+                dst, recv_sem = kvg_at(k // 2 * 2 + b, 0, col, h)
+                send(
+                    z_sum.at[(col + k + b) % 2, half(h)],
+                    dst,
+                    recv_sem,
+                    ctx_of(o_me, inner_of(k)),
+                    pair,
+                )
+        for b in range(2):
+            kvg[b * pairs, col, half(h)] = z_sum[(col + b) % 2, half(h)]
+            pass_on(b, col, h)
+
+    def kvg_forward(h):
+        for b in range(2):
+            landed(*kvg_at(b, 0, other, h))
+            pass_on(b, other, h)
+        for b in (2, 3):
+            for s in range(seqs):
+                landed(*kvg_at(b, 0, s, h))
+                pass_on(b, s, h)
+
+    def x_turn(chosen):
+        for n, (k, e) in enumerate(slots):
+            if k == chosen:
+                for o in range(x_parts):
+                    if n:
+                        landed(x_target(n, o), x_recv.at[n - 1, o])
+                    else:
+                        own_copies[o].wait()
+                cut = slice(n * seqs * rows, (n + 1) * seqs * rows)
+                for o in range(outer):
+                    xt[o, :, cut] = xg[n, o].T
+
+    x_start(3)
+    x_start(1)
     wait_half(0)
-    landed(q_in, swap_recv.at[0])
-    landed(g_in, swap_recv.at[1])
-    landed(delta_in, swap_recv.at[2])
-    x_start(1)
+    landed(delta_in, side_recv.at[0])
     for g in range(GROUPS):
+        cut = pl.ds(g * step, step)
+        landed(q_in.at[cut], swap_recv.at[g, 0])
+        landed(g_in.at[cut], swap_recv.at[g, 1])
         if g == GROUPS // HALVES:
             wait_half(1)
-            x_start(2)
+            x_start(2, 0, (x_parts + 1) // 2)
         attend(g)
         if g >= 1:
             y_start(g - 1)
         if g >= 2:
             z_start(g - 2)
     y_start(GROUPS - 1)
-    send(dq_out, dq_in, swap_recv.at[3], side, pair)
+    send(dq_out, dq_in, side_recv.at[1], side, pair)
+    x_start(2, (x_parts + 1) // 2)
     z_start(GROUPS - 2)
     z_start(GROUPS - 1)
-    x_start(3)
-    for b in range(GROUPS):
-        z_finish(b)
-
-    def kvg_at(k, e, s):
-        return kvg.at[k * pairs + e, s], kvg_recv.at[k * pairs + e, s]
-
-    def pass_on(k, s):
-        for e in range(1, pairs):
-            dst, recv_sem = kvg_at(k, e, s)
-            send(kvg_at(k, 0, s)[0], dst, recv_sem, me, (pair + e) % pairs)
-
-    for k in range(1, INNER):
-        for b in range(2):
-            dst, recv_sem = kvg_at(k // 2 * 2 + b, 0, col)
-            send(
-                z_sum.at[(col + k + b) % 2],
-                dst,
-                recv_sem,
-                ctx_of(o_me, inner_of(k)),
-                pair,
-            )
-    for b in range(2):
-        kvg[b * pairs, col] = z_sum[(col + b) % 2]
-        pass_on(b, col)
-    for b in range(2):
-        landed(*kvg_at(b, 0, other))
-        pass_on(b, other)
-    for b in (2, 3):
-        for s in range(seqs):
-            landed(*kvg_at(b, 0, s))
-            pass_on(b, s)
-
-    landed(dq_in, swap_recv.at[3])
+    x_turn(0)
+    z_finish(0)
+    z_finish(1)
+    kvg_start(0)
+    z_finish(2)
+    z_finish(3)
+    kvg_start(1)
+    x_turn(1)
+    kvg_forward(0)
+    x_turn(3)
+    kvg_forward(1)
+    x_turn(2)
+    landed(dq_in, side_recv.at[1])
     dq_ref[other] = dq_in[...]
-    for copy in own_copies:
-        copy.wait()
-    for n in range(1, len(slots)):
-        for o in range(x_parts):
-            landed(x_target(n, o), x_recv.at[n - 1, o])
-    for k in range(INNER):
-        for e in range(1, pairs):
-            for s in range(seqs):
-                landed(*kvg_at(k, e, s))
+    for h in range(HALVES):
+        for k in range(INNER):
+            for e in range(1, pairs):
+                for s in range(seqs):
+                    landed(*kvg_at(k, e, s, h))
 
     depth = len(slots) * seqs * rows
     kv_grads = kvg[...].reshape(depth, 2 * head)
-    for o in range(outer):
-        wsum[o] = dot(xg[:, o].reshape(depth, xg.shape[3]), kv_grads, 0, 0)
     for m in range(1, outer):
-        w_out[m - 1] = wsum[outer_of(m)].astype(jnp.bfloat16)
+        w_out[m - 1] = dot(xt[outer_of(m)], kv_grads, 1, 0).astype(jnp.bfloat16)
         send(
             w_out.at[m - 1], w_in.at[m - 1], w_recv.at[m - 1], ctx_of(outer_of(m), i_me), pair
         )
-    total = wsum[o_me]
+    wsum[...] = dot(xt[o_me], kv_grads, 1, 0)
+    total = wsum[...]
     for m in range(1, outer):
         landed(w_in.at[m - 1], w_recv.at[m - 1])
         total += w_in[m - 1].astype(jnp.float32)
@@ -417,7 +442,8 @@
         flat = jnp.pad(flat, ((0, 0), (0, 0), (0, 0), (0, padded - width)))
     vmem = pl.BlockSpec(memory_space=pltpu.VMEM)
     both = 2 * head
-    sends = HALVES * (4 * outer + 1) + 4 + GROUPS * outer + 6 + 8 * (pairs - 1)
+    sends = HALVES * (4 * outer + 1) + 2 * GROUPS + 2 + GROUPS * outer
+    sends += HALVES * (6 + 8 * (pairs - 1))
     sends += (slots - 1) * x_parts + (outer - 1) + (pairs - 1)
     dma = pltpu.SemaphoreType.DMA
     f32, bf16 = jnp.float32, jnp.bfloat16
@@ -452,16 +478,18 @@
             pltpu.VMEM((2, rows, both), bf16),
             pltpu.VMEM((slots, seqs, rows, both), bf16),
             pltpu.VMEM((slots, outer, flat_rows, padded), bf16),
-            pltpu.VMEM((outer, padded, both), f32),
+            pltpu.VMEM((outer, padded, slots * flat_rows), bf16),
+            pltpu.VMEM((padded, both), f32),
             pltpu.VMEM((outer - 1, padded, both), bf16),
             pltpu.VMEM((outer - 1, padded, both), bf16),
             pltpu.VMEM((pairs, width, both), f32),
             dma((sends,)),
-            dma((4,)),
+            dma((GROUPS, 2)),
+            dma((2,)),
             dma((HALVES, ctx)),
             dma((GROUPS,)),
             dma((GROUPS, outer - 1)),
-            dma((slots, seqs)),
+            dma((HALVES, slots, seqs)),
             dma((slots - 1, x_parts)),
             dma((outer - 1,)),
             dma((pairs - 1,)),

time: 55.1 us -> 56.5 us (1.025)
  Pallas kernels: 51.8 us -> 53.3 us
    pallas_call x1, Pallas kernels: 51.8 us -> 53.3 us  [local(): pl.pallas_call(functools.partial(kernel, (outer, pairs, width)), out_shap...]
where the time goes in v3:
time: 56.5 us; the launch traced here: 56.4 us
  Pallas kernels  53.3 us (94%)
  local copies, waits for them, and re-layouts  2.42 us (4%)
  between operations  0.65 us (1%)
    pallas_call x1, Pallas kernels, local(): pl.pallas_call(functools.partial(kernel, (outer, pairs, width)), out_shap...  53.3 us
    unnamed x4, local copies, waits for them, and re-layouts  2.42 us

profile of v3, /device:TPU:0, one launch (start us, length us, event | category | flops | bytes accessed | tf_op | source)
XLA Modules:
  0.0 56.4 jit_solution(851906296053804263)
XLA Ops:
  0.6 53.3 %shard_map.95 = (bf16[2,64,1024]{2,1,0:T(8,128)(2,1)}, f32[256,256]{1,0:T(8,128)}) custom-call(bf16[128,4096]{1,0:T(8,128)(2,1)} %bitcast.1, bf16[2,64,1024]{2,1,0:T(8,128)(2,1)} %q_ref.1, bf16[2,64,128]{2,1,0:T(8,128)(2,1)} %k_ref.1, bf16[2,64,128]{2,1,0:T(8,128)(2,1)} %v_ref.1, bf16[2,64,1024]{2,1,0:T(8,128)(2,1)} %a_ref.1, bf16[2,64,1024]{2,1,0:T(8,128)(2,1)} %g_ref.1, ...), custom_call_target="tpu_custom_call" | custom-call | tf_op jit(solution)/shard_map/pallas_call | solution.py:452
  53.9 0.0 copy-start
  53.9 1.7 %copy.12 = bf16[2,64,1024]{2,1,0:T(8,128)(2,1)} copy(bf16[2,64,1024]{2,1,0:T(8,128)(2,1)} %get-tuple-element.4) | data formatting | bytes 524288
  55.7 0.0 copy-done
  55.7 0.7 %copy.13 = f32[256,256]{1,0:T(8,128)} copy(f32[256,256]{1,0:T(8,128)S(1)} %copy-done) | data formatting | bytes 524288
Async XLA Ops:
  53.9 1.7 %copy-start = (f32[256,256]{1,0:T(8,128)S(1)}, f32[256,256]{1,0:T(8,128)}, u32[]{:S(2)}) copy-start(f32[256,256]{1,0:T(8,128)} %get-tuple-element.5) | copy-start | bytes 786436

commit v4 on v3

--- a/solution.py
+++ b/solution.py
@@ -57,6 +57,7 @@
     send_sem,
     swap_recv,
     side_recv,
+    kv_recv,
     ag_recv,
     y_recv,
     z_recv,
@@ -145,17 +146,16 @@
     def half(h):
         return pl.ds(h * (rows // HALVES), rows // HALVES)
 
-    def block_send(src, h, ctx):
-        send(kv.at[src, half(h)], kv.at[src, half(h)], ag_recv.at[h, src], ctx, pair)
-
-    def block_landed(src, h):
-        landed(kv.at[src, half(h)], ag_recv.at[h, src])
+    def both_of(o, r, h):
+        blocks = kv.at[pl.ds(ctx_of(o, 2 * r), 2), half(h)]
+        return blocks, ag_recv.at[h, o * 2 + r]
+
+    def both_send(o, h, ctx):
+        blocks, recv_sem = both_of(o, row, h)
+        send(blocks, blocks, recv_sem, ctx, pair)
 
     for h in range(HALVES):
-        send(kv_swap.at[half(h)], kv.at[me, half(h)], ag_recv.at[h, me], side, pair)
-        for m in range(1, outer):
-            block_send(me, h, ctx_of(outer_of(m), i_me))
-        block_send(me, h, across)
+        send(kv_swap.at[half(h)], kv.at[me, half(h)], kv_recv.at[h], side, pair)
     for g in range(GROUPS):
         cut = pl.ds(g * step, step)
         send(q_ref.at[other, cut], q_in.at[cut], swap_recv.at[g, 0], side, pair)
@@ -166,13 +166,16 @@
             return x_ref.at[:, pl.ds(pl.multiple_of(first, LANES), width)]
         return x_ref.at[i * pairs + d]
 
+    def slot_of(k, e, column):
+        return (e * 2 + k // 2) * 2 + (column + k % 2) % 2
+
     def x_target(n, o):
         return xg.at[n, o] if x_ref.ndim == 2 else xg.at[n]
 
     own_copies = []
     for o in range(x_parts):
         own_copies.append(
-            pltpu.make_async_copy(x_source(o, i_me, pair), x_target(0, o), own_sem.at[o])
+            pltpu.make_async_copy(x_source(o, i_me, pair), x_target(slot_of(0, 0, col), o), own_sem.at[o])
         )
         own_copies[-1].start()
 
@@ -182,7 +185,7 @@
                 for o in range(first, last):
                     send(
                         x_source(o, inner_of(k), (pair + e) % pairs),
-                        x_target(n, o),
+                        x_target(slot_of(k - k % 2, e, col), o),
                         x_recv.at[n - 1, o],
                         ctx_of(o_me, inner_of(k)),
                         (pair + e) % pairs,
@@ -190,10 +193,10 @@
 
     x_start(0)
     for h in range(HALVES):
-        block_landed(side, h)
+        landed(kv.at[side, half(h)], kv_recv.at[h])
         for m in range(1, outer):
-            block_send(side, h, ctx_of(outer_of(m), i_me))
-        block_send(side, h, across)
+            both_send(o_me, h, ctx_of(outer_of(m), i_me))
+        both_send(o_me, h, across)
 
     for g in range(GROUPS):
         delta_out[g : g + 1, :] = delta_rows(other, g)
@@ -201,9 +204,8 @@
     def forward(h):
         for m in range(1, outer):
             o = outer_of(outer - m)
-            for src in (ctx_of(o, i_me), ctx_of(o, inner_of(1))):
-                block_landed(src, h)
-                block_send(src, h, across)
+            landed(*both_of(o, row, h))
+            both_send(o, h, across)
 
     forward(0)
     for g in range(GROUPS):
@@ -222,24 +224,28 @@
         dcol[cut] = columns_of(doc_line[:, cut])
 
     forward(1)
+    own_rows = jnp.concatenate([kpos[me], kpos[side]], axis=0)
+    sub = lax.broadcasted_iota(jnp.int32, own_rows.shape, 0)
+    lane = lax.broadcasted_iota(jnp.int32, own_rows.shape, 1)
+    row_pos = jnp.sum(jnp.where(sub == lane, own_rows, 0.0), axis=0, keepdims=True)
     place = lax.broadcasted_iota(jnp.int32, (total_rows, LANES), 0).astype(jnp.float32)
-    sub = lax.broadcasted_iota(jnp.int32, (step, LANES), 0)
-    lane = lax.broadcasted_iota(jnp.int32, (step, LANES), 1)
-    pick = sub == lane % step
     doc_cols = dcol[...]
-
-    def query_row(g, src):
-        own = kpos[src, g * step : (g + 1) * step, :]
-        pos = jnp.sum(jnp.where(pick, own, 0.0), axis=0, keepdims=True)
-        doc = jnp.sum(jnp.where(place == pos, doc_cols, 0.0), axis=0, keepdims=True)
-        first = jnp.sum(jnp.where(doc_cols < doc, 1.0, 0.0), axis=0, keepdims=True)
-        return pos, first
+    row_doc = jnp.sum(jnp.where(place == row_pos, doc_cols, 0.0), axis=0, keepdims=True)
+    row_first = jnp.sum(jnp.where(doc_cols < row_doc, 1.0, 0.0), axis=0, keepdims=True)
+    first_rows = columns_of(row_first)
+    pick = (sub == lane % step)[:step]
+
+    def along(block):
+        return jnp.sum(jnp.where(pick, block, 0.0), axis=0, keepdims=True)
 
     found = []
     for g in range(GROUPS):
-        own_row, side_row = query_row(g, me), query_row(g, side)
+        places = [slice(n * rows + g * step, n * rows + (g + 1) * step) for n in range(2)]
         found.append(
-            tuple(jnp.concatenate([a, b], axis=1) for a, b in zip(own_row, side_row))
+            tuple(
+                jnp.concatenate([along(block[cut]) for cut in places], axis=1)
+                for block in (own_rows, first_rows)
+            )
         )
 
     def dot(a, b, ca, cb):
@@ -253,6 +259,7 @@
         span = high - low
         key_count = ctx_count * span
         cut = slice(g * step, (g + 1) * step)
+        own_cut = pl.ds(pl.multiple_of(col * rows + g * step, step), step)
         key_block = kv[:, low:high, 0:head].reshape(key_count, head)
         value_block = kv[:, low:high, head : 2 * head].reshape(key_count, head)
         key_pos = kpos[:, low:high, :].reshape(key_count, LANES)
@@ -275,7 +282,7 @@
         query_grad = (dot(score_grad, key_block, 0, 0) * scale).astype(jnp.bfloat16)
         for h in range(heads):
             cols = slice(h * head, (h + 1) * head)
-            dq_ref[col, cut, cols] = query_grad[h * step : (h + 1) * step]
+            dq_ref[own_cut, cols] = query_grad[h * step : (h + 1) * step]
             dq_out[cut, cols] = query_grad[(heads + h) * step : (heads + h + 1) * step]
         for part, grad in ((0, key_grad), (1, value_grad)):
             grad = grad.reshape(outer, 2, 2, span, head)
@@ -310,53 +317,39 @@
 
     def wait_half(h):
         for o in range(outer):
-            for k in (2, 3):
-                block_landed(ctx_of(outer_of(o), inner_of(k)), h)
-
-    def kvg_at(k, e, s, h):
-        slot = k * pairs + e
-        return kvg.at[slot, s, half(h)], kvg_recv.at[h, slot, s]
-
-    def pass_on(k, s, h):
+            landed(*both_of(outer_of(o), (row + 1) % 2, h))
+
+    def kvg_at(r, e, s):
+        return kvg.at[e, pl.ds(2 * r, 2), s], kvg_recv.at[e, r, s]
+
+    def pass_on(r, s):
         for e in range(1, pairs):
-            dst, recv_sem = kvg_at(k, e, s, h)
-            send(kvg_at(k, 0, s, h)[0], dst, recv_sem, me, (pair + e) % pairs)
-
-    def kvg_start(h):
+            dst, recv_sem = kvg_at(r, e, s)
+            send(kvg_at(r, 0, s)[0], dst, recv_sem, me, (pair + e) % pairs)
+
+    def kvg_start():
         for k in range(1, INNER):
-            for b in range(2):
-                dst, recv_sem = kvg_at(k // 2 * 2 + b, 0, col, h)
-                send(
-                    z_sum.at[(col + k + b) % 2, half(h)],
-                    dst,
-                    recv_sem,
-                    ctx_of(o_me, inner_of(k)),
-                    pair,
-                )
-        for b in range(2):
-            kvg[b * pairs, col, half(h)] = z_sum[(col + b) % 2, half(h)]
-            pass_on(b, col, h)
-
-    def kvg_forward(h):
-        for b in range(2):
-            landed(*kvg_at(b, 0, other, h))
-            pass_on(b, other, h)
-        for b in (2, 3):
-            for s in range(seqs):
-                landed(*kvg_at(b, 0, s, h))
-                pass_on(b, s, h)
+            dst, recv_sem = kvg_at(k // 2, 0, col)
+            send(z_sum, dst, recv_sem, ctx_of(o_me, inner_of(k)), pair)
+        kvg[0, 0:2, col] = z_sum[...]
+        pass_on(0, col)
+
+    def kvg_forward(r, s):
+        landed(*kvg_at(r, 0, s))
+        pass_on(r, s)
 
     def x_turn(chosen):
         for n, (k, e) in enumerate(slots):
             if k == chosen:
                 for o in range(x_parts):
                     if n:
-                        landed(x_target(n, o), x_recv.at[n - 1, o])
+                        landed(x_target(slot_of(k, e, col), o), x_recv.at[n - 1, o])
                     else:
                         own_copies[o].wait()
-                cut = slice(n * seqs * rows, (n + 1) * seqs * rows)
+                slot = slot_of(k, e, col)
+                cut = pl.ds(pl.multiple_of(slot * (seqs * rows), seqs * rows), seqs * rows)
                 for o in range(outer):
-                    xt[o, :, cut] = xg[n, o].T
+                    xt[o, :, cut] = xg[slot, o].T
 
     x_start(3)
     x_start(1)
@@ -380,24 +373,21 @@
     z_start(GROUPS - 2)
     z_start(GROUPS - 1)
     x_turn(0)
-    z_finish(0)
-    z_finish(1)
-    kvg_start(0)
-    z_finish(2)
-    z_finish(3)
-    kvg_start(1)
     x_turn(1)
-    kvg_forward(0)
+    for b in range(GROUPS):
+        z_finish(b)
+    kvg_start()
     x_turn(3)
-    kvg_forward(1)
+    kvg_forward(0, other)
+    kvg_forward(1, col)
+    kvg_forward(1, other)
     x_turn(2)
     landed(dq_in, side_recv.at[1])
-    dq_ref[other] = dq_in[...]
-    for h in range(HALVES):
-        for k in range(INNER):
-            for e in range(1, pairs):
-                for s in range(seqs):
-                    landed(*kvg_at(k, e, s, h))
+    dq_ref[pl.ds(pl.multiple_of(other * rows, rows), rows), :] = dq_in[...]
+    for e in range(1, pairs):
+        for r in range(2):
+            for s in range(seqs):
+                landed(*kvg_at(r, e, s))
 
     depth = len(slots) * seqs * rows
     kv_grads = kvg[...].reshape(depth, 2 * head)
@@ -442,17 +432,16 @@
         flat = jnp.pad(flat, ((0, 0), (0, 0), (0, 0), (0, padded - width)))
     vmem = pl.BlockSpec(memory_space=pltpu.VMEM)
     both = 2 * head
-    sends = HALVES * (4 * outer + 1) + 2 * GROUPS + 2 + GROUPS * outer
-    sends += HALVES * (6 + 8 * (pairs - 1))
+    sends = HALVES * 2 * outer + 2 * GROUPS + 2 + GROUPS * outer + 3 + 4 * (pairs - 1)
     sends += (slots - 1) * x_parts + (outer - 1) + (pairs - 1)
     dma = pltpu.SemaphoreType.DMA
     f32, bf16 = jnp.float32, jnp.bfloat16
     step = rows // GROUPS
     query_width = queries.shape[2]
-    return pl.pallas_call(
+    query_grad, weight_grad = pl.pallas_call(
         functools.partial(kernel, (outer, pairs, width)),
         out_shape=(
-            jax.ShapeDtypeStruct(queries.shape, bf16),
+            jax.ShapeDtypeStruct((flat_rows, query_width), bf16),
             jax.ShapeDtypeStruct((model // ctx, both), f32),
         ),
         in_specs=[pl.BlockSpec(memory_space=pl.ANY)] + [vmem] * 7,
@@ -476,7 +465,7 @@
             pltpu.VMEM((GROUPS, outer - 1, 2, step, both), bf16),
             pltpu.VMEM((GROUPS, outer - 1, 2, step, both), bf16),
             pltpu.VMEM((2, rows, both), bf16),
-            pltpu.VMEM((slots, seqs, rows, both), bf16),
+            pltpu.VMEM((pairs, INNER, seqs, rows, both), bf16),
             pltpu.VMEM((slots, outer, flat_rows, padded), bf16),
             pltpu.VMEM((outer, padded, slots * flat_rows), bf16),
             pltpu.VMEM((padded, both), f32),
@@ -486,10 +475,11 @@
             dma((sends,)),
             dma((GROUPS, 2)),
             dma((2,)),
-            dma((HALVES, ctx)),
+            dma((HALVES,)),
+            dma((HALVES, 2 * outer)),
             dma((GROUPS,)),
             dma((GROUPS, outer - 1)),
-            dma((HALVES, slots, seqs)),
+            dma((pairs, 2, seqs)),
             dma((slots - 1, x_parts)),
             dma((outer - 1,)),
             dma((pairs - 1,)),
@@ -499,6 +489,7 @@
             collective_id=0, has_side_effects=True, vmem_limit_bytes=60 * 1024 * 1024
         ),
     )(flat, queries, key_states, value_states, attn_output, out_grad, doc_ids, positions)
+    return query_grad.reshape(queries.shape), weight_grad
 
 
 def solution(mesh):

time: 56.5 us -> 57.7 us (1.021)
  Pallas kernels: 53.3 us -> 54.5 us
    pallas_call x1, Pallas kernels: 53.3 us -> 54.5 us  [local(): pl.pallas_call(functools.partial(kernel, (outer, pairs, width)), out_shap...]
where the time goes in v4:
time: 57.7 us; the launch traced here: 57.6 us
  Pallas kernels  54.5 us (94%)
  local copies, waits for them, and re-layouts  2.42 us (4%)
  between operations  0.65 us (1%)
    pallas_call x1, Pallas kernels, local(): pl.pallas_call(functools.partial(kernel, (outer, pairs, width)), out_shap...  54.5 us
    unnamed x4, local copies, waits for them, and re-layouts  2.42 us

profile of v4, /device:TPU:0, one launch (start us, length us, event | category | flops | bytes accessed | tf_op | source)
XLA Modules:
  0.0 57.6 jit_solution(7709829548839567653)
XLA Ops:
  0.6 54.5 %shard_map.95 = (bf16[128,1024]{1,0:T(8,128)(2,1)}, f32[256,256]{1,0:T(8,128)}) custom-call(bf16[128,4096]{1,0:T(8,128)(2,1)} %bitcast.2, bf16[2,64,1024]{2,1,0:T(8,128)(2,1)} %q_ref.1, bf16[2,64,128]{2,1,0:T(8,128)(2,1)} %k_ref.1, bf16[2,64,128]{2,1,0:T(8,128)(2,1)} %v_ref.1, bf16[2,64,1024]{2,1,0:T(8,128)(2,1)} %a_ref.1, bf16[2,64,1024]{2,1,0:T(8,128)(2,1)} %g_ref.1, ...), custom_call_target="tpu_custom_call" | custom-call | tf_op jit(solution)/shard_map/pallas_call | solution.py:441
  55.1 0.0 copy-start
  55.2 1.7 %copy.12 = bf16[2,64,1024]{2,1,0:T(8,128)(2,1)} copy(bf16[2,64,1024]{2,1,0:T(8,128)(2,1)} %bitcast.3) | data formatting | bytes 524288
  56.9 0.0 copy-done
  56.9 0.7 %copy.13 = f32[256,256]{1,0:T(8,128)} copy(f32[256,256]{1,0:T(8,128)S(1)} %copy-done) | data formatting | bytes 524288
Async XLA Ops:
  55.1 1.7 %copy-start = (f32[256,256]{1,0:T(8,128)S(1)}, f32[256,256]{1,0:T(8,128)}, u32[]{:S(2)}) copy-start(f32[256,256]{1,0:T(8,128)} %get-tuple-element.9) | copy-start | bytes 786436

commit v5 on v4

--- a/solution.py
+++ b/solution.py
@@ -51,18 +51,20 @@
     xg,
     xt,
     wsum,
+    wy_out,
+    wy_in,
     w_out,
     w_in,
     w_fin,
     send_sem,
     swap_recv,
     side_recv,
-    kv_recv,
     ag_recv,
     y_recv,
     z_recv,
     kvg_recv,
     x_recv,
+    wy_recv,
     w_recv,
     fin_recv,
     own_sem,
@@ -72,7 +74,7 @@
     heads = q_ref.shape[2] // head
     step = rows // GROUPS
     scale = 1.0 / math.sqrt(head)
-    x_parts = outer if x_ref.ndim == 2 else 1
+    x_parts = 2 * outer if x_ref.ndim == 2 else 1
     ctx_count = outer * INNER
 
     me = lax.axis_index("ctx")
@@ -112,10 +114,11 @@
     def landed(dst, recv_sem):
         copy_to(dst, dst, recv_sem, side, pair, 0).wait_recv()
 
-    slots = [(k, e) for k in range(INNER) for e in range(pairs)]
+    slots = [(k, e) for k in range(2) for e in range(pairs)]
 
     barrier = pltpu.get_barrier_semaphore()
     greeted = [(ctx_of(outer_of(m), i_me), pair) for m in range(1, outer)]
+    greeted += [(across, pair)]
     greeted += [(ctx_of(o_me, inner_of(k)), (pair + e) % pairs) for k, e in slots[1:]]
     for ctx, dp in greeted:
         pl.semaphore_signal(
@@ -146,28 +149,29 @@
     def half(h):
         return pl.ds(h * (rows // HALVES), rows // HALVES)
 
-    def both_of(o, r, h):
-        blocks = kv.at[pl.ds(ctx_of(o, 2 * r), 2), half(h)]
-        return blocks, ag_recv.at[h, o * 2 + r]
-
-    def both_send(o, h, ctx):
-        blocks, recv_sem = both_of(o, row, h)
-        send(blocks, blocks, recv_sem, ctx, pair)
+    def block_send(src, h, ctx):
+        send(kv.at[src, half(h)], kv.at[src, half(h)], ag_recv.at[h, src], ctx, pair)
+
+    def block_landed(src, h):
+        landed(kv.at[src, half(h)], ag_recv.at[h, src])
 
     for h in range(HALVES):
-        send(kv_swap.at[half(h)], kv.at[me, half(h)], kv_recv.at[h], side, pair)
+        send(kv_swap.at[half(h)], kv.at[me, half(h)], ag_recv.at[h, me], side, pair)
+        for m in range(1, outer):
+            block_send(me, h, ctx_of(outer_of(m), i_me))
+        block_send(me, h, across)
     for g in range(GROUPS):
         cut = pl.ds(g * step, step)
         send(q_ref.at[other, cut], q_in.at[cut], swap_recv.at[g, 0], side, pair)
         send(g_ref.at[other, cut], g_in.at[cut], swap_recv.at[g, 1], side, pair)
     def x_source(o, i, d):
         if x_ref.ndim == 2:
-            first = (ctx_of(o, i) * pairs + d) * width
+            first = ((o * 2 + i) * pairs + d) * width
             return x_ref.at[:, pl.ds(pl.multiple_of(first, LANES), width)]
         return x_ref.at[i * pairs + d]
 
     def slot_of(k, e, column):
-        return (e * 2 + k // 2) * 2 + (column + k % 2) % 2
+        return e * 2 + (column + k) % 2
 
     def x_target(n, o):
         return xg.at[n, o] if x_ref.ndim == 2 else xg.at[n]
@@ -175,17 +179,17 @@
     own_copies = []
     for o in range(x_parts):
         own_copies.append(
-            pltpu.make_async_copy(x_source(o, i_me, pair), x_target(slot_of(0, 0, col), o), own_sem.at[o])
+            pltpu.make_async_copy(x_source(o, col, pair), x_target(slot_of(0, 0, col), o), own_sem.at[o])
         )
         own_copies[-1].start()
 
-    def x_start(chosen, first=0, last=x_parts):
+    def x_start(chosen):
         for n, (k, e) in enumerate(slots):
             if n and k == chosen:
-                for o in range(first, last):
+                for o in range(x_parts):
                     send(
-                        x_source(o, inner_of(k), (pair + e) % pairs),
-                        x_target(slot_of(k - k % 2, e, col), o),
+                        x_source(o, (col + k) % 2, (pair + e) % pairs),
+                        x_target(slot_of(0, e, col), o),
                         x_recv.at[n - 1, o],
                         ctx_of(o_me, inner_of(k)),
                         (pair + e) % pairs,
@@ -193,10 +197,10 @@
 
     x_start(0)
     for h in range(HALVES):
-        landed(kv.at[side, half(h)], kv_recv.at[h])
+        block_landed(side, h)
         for m in range(1, outer):
-            both_send(o_me, h, ctx_of(outer_of(m), i_me))
-        both_send(o_me, h, across)
+            block_send(side, h, ctx_of(outer_of(m), i_me))
+        block_send(side, h, across)
 
     for g in range(GROUPS):
         delta_out[g : g + 1, :] = delta_rows(other, g)
@@ -204,8 +208,9 @@
     def forward(h):
         for m in range(1, outer):
             o = outer_of(outer - m)
-            landed(*both_of(o, row, h))
-            both_send(o, h, across)
+            for src in (ctx_of(o, i_me), ctx_of(o, inner_of(1))):
+                block_landed(src, h)
+                block_send(src, h, across)
 
     forward(0)
     for g in range(GROUPS):
@@ -317,26 +322,16 @@
 
     def wait_half(h):
         for o in range(outer):
-            landed(*both_of(outer_of(o), (row + 1) % 2, h))
-
-    def kvg_at(r, e, s):
-        return kvg.at[e, pl.ds(2 * r, 2), s], kvg_recv.at[e, r, s]
-
-    def pass_on(r, s):
+            for k in (2, 3):
+                block_landed(ctx_of(outer_of(o), inner_of(k)), h)
+
+    def kvg_at(e, s):
+        return kvg.at[e, :, s], kvg_recv.at[e, s]
+
+    def pass_on(s):
         for e in range(1, pairs):
-            dst, recv_sem = kvg_at(r, e, s)
-            send(kvg_at(r, 0, s)[0], dst, recv_sem, me, (pair + e) % pairs)
-
-    def kvg_start():
-        for k in range(1, INNER):
-            dst, recv_sem = kvg_at(k // 2, 0, col)
-            send(z_sum, dst, recv_sem, ctx_of(o_me, inner_of(k)), pair)
-        kvg[0, 0:2, col] = z_sum[...]
-        pass_on(0, col)
-
-    def kvg_forward(r, s):
-        landed(*kvg_at(r, 0, s))
-        pass_on(r, s)
+            dst, recv_sem = kvg_at(e, s)
+            send(kvg_at(0, s)[0], dst, recv_sem, me, (pair + e) % pairs)
 
     def x_turn(chosen):
         for n, (k, e) in enumerate(slots):
@@ -348,11 +343,9 @@
                         own_copies[o].wait()
                 slot = slot_of(k, e, col)
                 cut = pl.ds(pl.multiple_of(slot * (seqs * rows), seqs * rows), seqs * rows)
-                for o in range(outer):
+                for o in range(2 * outer):
                     xt[o, :, cut] = xg[slot, o].T
 
-    x_start(3)
-    x_start(1)
     wait_half(0)
     landed(delta_in, side_recv.at[0])
     for g in range(GROUPS):
@@ -361,43 +354,47 @@
         landed(g_in.at[cut], swap_recv.at[g, 1])
         if g == GROUPS // HALVES:
             wait_half(1)
-            x_start(2, 0, (x_parts + 1) // 2)
         attend(g)
+        if g == 0:
+            x_start(1)
         if g >= 1:
             y_start(g - 1)
         if g >= 2:
             z_start(g - 2)
     y_start(GROUPS - 1)
     send(dq_out, dq_in, side_recv.at[1], side, pair)
-    x_start(2, (x_parts + 1) // 2)
     z_start(GROUPS - 2)
     z_start(GROUPS - 1)
     x_turn(0)
-    x_turn(1)
     for b in range(GROUPS):
         z_finish(b)
-    kvg_start()
-    x_turn(3)
-    kvg_forward(0, other)
-    kvg_forward(1, col)
-    kvg_forward(1, other)
-    x_turn(2)
+    dst, recv_sem = kvg_at(0, col)
+    send(z_sum, dst, recv_sem, side, pair)
+    kvg[0, :, col] = z_sum[...]
+    pass_on(col)
+    x_turn(1)
+    landed(*kvg_at(0, other))
+    pass_on(other)
     landed(dq_in, side_recv.at[1])
     dq_ref[pl.ds(pl.multiple_of(other * rows, rows), rows), :] = dq_in[...]
     for e in range(1, pairs):
-        for r in range(2):
-            for s in range(seqs):
-                landed(*kvg_at(r, e, s))
+        for s in range(seqs):
+            landed(*kvg_at(e, s))
 
     depth = len(slots) * seqs * rows
     kv_grads = kvg[...].reshape(depth, 2 * head)
-    for m in range(1, outer):
-        w_out[m - 1] = dot(xt[outer_of(m)], kv_grads, 1, 0).astype(jnp.bfloat16)
-        send(
-            w_out.at[m - 1], w_in.at[m - 1], w_recv.at[m - 1], ctx_of(outer_of(m), i_me), pair
-        )
-    wsum[...] = dot(xt[o_me], kv_grads, 1, 0)
-    total = wsum[...]
+    for n in range(outer):
+        o = outer_of((n + 1) % outer)
+        wy_out[n] = dot(xt[o * 2 + (row + 1) % 2], kv_grads, 1, 0).astype(jnp.bfloat16)
+        send(wy_out.at[n], wy_in.at[n], wy_recv.at[n], across, pair)
+    for n in range(outer):
+        wsum[n] = dot(xt[outer_of((n + 1) % outer) * 2 + row], kv_grads, 1, 0)
+    for n in range(outer):
+        landed(wy_in.at[n], wy_recv.at[n])
+        total = wsum[n] + wy_in[n].astype(jnp.float32)
+        if n < outer - 1:
+            w_out[n] = total.astype(jnp.bfloat16)
+            send(w_out.at[n], w_in.at[n], w_recv.at[n], ctx_of(outer_of(n + 1), i_me), pair)
     for m in range(1, outer):
         landed(w_in.at[m - 1], w_recv.at[m - 1])
         total += w_in[m - 1].astype(jnp.float32)
@@ -421,19 +418,19 @@
     outer = ctx // INNER
     width = model // (ctx * pairs)
     padded = -(-width // LANES) * LANES
-    slots = INNER * pairs
+    slots = 2 * pairs
     flat_rows = seqs * rows
     flat = layer_input.reshape(flat_rows, model)
     if padded == width:
-        x_parts = outer
+        x_parts = 2 * outer
     else:
         x_parts = 1
-        flat = flat.reshape(flat_rows, outer, INNER * pairs, width).transpose(2, 1, 0, 3)
+        flat = flat.reshape(flat_rows, 2 * outer, 2 * pairs, width).transpose(2, 1, 0, 3)
         flat = jnp.pad(flat, ((0, 0), (0, 0), (0, 0), (0, padded - width)))
     vmem = pl.BlockSpec(memory_space=pltpu.VMEM)
     both = 2 * head
-    sends = HALVES * 2 * outer + 2 * GROUPS + 2 + GROUPS * outer + 3 + 4 * (pairs - 1)
-    sends += (slots - 1) * x_parts + (outer - 1) + (pairs - 1)
+    sends = HALVES * (4 * outer + 1) + 2 * GROUPS + 2 + GROUPS * outer + 1 + 2 * (pairs - 1)
+    sends += (slots - 1) * x_parts + outer + (outer - 1) + (pairs - 1)
     dma = pltpu.SemaphoreType.DMA
     f32, bf16 = jnp.float32, jnp.bfloat16
     step = rows // GROUPS
@@ -465,22 +462,24 @@
             pltpu.VMEM((GROUPS, outer - 1, 2, step, both), bf16),
             pltpu.VMEM((GROUPS, outer - 1, 2, step, both), bf16),
             pltpu.VMEM((2, rows, both), bf16),
-            pltpu.VMEM((pairs, INNER, seqs, rows, both), bf16),
-            pltpu.VMEM((slots, outer, flat_rows, padded), bf16),
-            pltpu.VMEM((outer, padded, slots * flat_rows), bf16),
-            pltpu.VMEM((padded, both), f32),
+            pltpu.VMEM((pairs, 2, seqs, rows, both), bf16),
+            pltpu.VMEM((slots, 2 * outer, flat_rows, padded), bf16),
+            pltpu.VMEM((2 * outer, padded, slots * flat_rows), bf16),
+            pltpu.VMEM((outer, padded, both), f32),
+            pltpu.VMEM((outer, padded, both), bf16),
+            pltpu.VMEM((outer, padded, both), bf16),
             pltpu.VMEM((outer - 1, padded, both), bf16),
             pltpu.VMEM((outer - 1, padded, both), bf16),
             pltpu.VMEM((pairs, width, both), f32),
             dma((sends,)),
             dma((GROUPS, 2)),
             dma((2,)),
-            dma((HALVES,)),
-            dma((HALVES, 2 * outer)),
+            dma((HALVES, ctx)),
             dma((GROUPS,)),
             dma((GROUPS, outer - 1)),
-            dma((pairs, 2, seqs)),
+            dma((pairs, seqs)),
             dma((slots - 1, x_parts)),
+            dma((outer,)),
             dma((outer - 1,)),
             dma((pairs - 1,)),
             dma((x_parts,)),

time: 57.7 us -> 51.8 us (0.90)
  Pallas kernels: 54.5 us -> 48.6 us
    pallas_call x1, Pallas kernels: 54.5 us -> 48.6 us  [local(): pl.pallas_call(functools.partial(kernel, (outer, pairs, width)), out_shap...]
where the time goes in v5:
time: 51.8 us; the launch traced here: 51.6 us
  Pallas kernels  48.6 us (94%)
  local copies, waits for them, and re-layouts  2.42 us (5%)
  between operations  0.65 us (1%)
    pallas_call x1, Pallas kernels, local(): pl.pallas_call(functools.partial(kernel, (outer, pairs, width)), out_shap...  48.6 us
    unnamed x4, local copies, waits for them, and re-layouts  2.42 us

profile of v5, /device:TPU:0, one launch (start us, length us, event | category | flops | bytes accessed | tf_op | source)
XLA Modules:
  0.0 51.6 jit_solution(13037470376671375598)
XLA Ops:
  0.6 48.6 %shard_map.95 = (bf16[128,1024]{1,0:T(8,128)(2,1)}, f32[256,256]{1,0:T(8,128)}) custom-call(bf16[128,4096]{1,0:T(8,128)(2,1)} %bitcast.2, bf16[2,64,1024]{2,1,0:T(8,128)(2,1)} %q_ref.1, bf16[2,64,128]{2,1,0:T(8,128)(2,1)} %k_ref.1, bf16[2,64,128]{2,1,0:T(8,128)(2,1)} %v_ref.1, bf16[2,64,1024]{2,1,0:T(8,128)(2,1)} %a_ref.1, bf16[2,64,1024]{2,1,0:T(8,128)(2,1)} %g_ref.1, ...), custom_call_target="tpu_custom_call" | custom-call | tf_op jit(solution)/shard_map/pallas_call | solution.py:438
  49.2 0.0 copy-start
  49.2 1.7 %copy.12 = bf16[2,64,1024]{2,1,0:T(8,128)(2,1)} copy(bf16[2,64,1024]{2,1,0:T(8,128)(2,1)} %bitcast.3) | data formatting | bytes 524288
  50.9 0.0 copy-done
  50.9 0.7 %copy.13 = f32[256,256]{1,0:T(8,128)} copy(f32[256,256]{1,0:T(8,128)S(1)} %copy-done) | data formatting | bytes 524288
Async XLA Ops:
  49.2 1.7 %copy-start = (f32[256,256]{1,0:T(8,128)S(1)}, f32[256,256]{1,0:T(8,128)}, u32[]{:S(2)}) copy-start(f32[256,256]{1,0:T(8,128)} %get-tuple-element.9) | copy-start | bytes 786436

commit v6 on v5

--- a/solution.py
+++ b/solution.py
@@ -176,6 +176,12 @@
     def x_target(n, o):
         return xg.at[n, o] if x_ref.ndim == 2 else xg.at[n]
 
+    def slot_of(k, e, column):
+        return e * 2 + (column + k) % 2
+
+    def x_target(n, o):
+        return xg.at[n, o] if x_ref.ndim == 2 else xg.at[n]
+
     own_copies = []
     for o in range(x_parts):
         own_copies.append(
@@ -195,7 +201,6 @@
                         (pair + e) % pairs,
                     )
 
-    x_start(0)
     for h in range(HALVES):
         block_landed(side, h)
         for m in range(1, outer):
@@ -229,6 +234,8 @@
         dcol[cut] = columns_of(doc_line[:, cut])
 
     forward(1)
+    x_start(0)
+
     own_rows = jnp.concatenate([kpos[me], kpos[side]], axis=0)
     sub = lax.broadcasted_iota(jnp.int32, own_rows.shape, 0)
     lane = lax.broadcasted_iota(jnp.int32, own_rows.shape, 1)
@@ -277,8 +284,9 @@
         )
         delta = jnp.concatenate([delta_own[g : g + 1, :], delta_in[g : g + 1, :]], axis=1)
         live = (key_pos <= pos) & (key_pos >= first)
-        scores = jnp.where(live, dot(key_block, query_n, 1, 1) * scale, NEG_FILL)
-        terms = jnp.exp(scores - jnp.max(scores, axis=0, keepdims=True))
+        scores = jnp.where(live, dot(key_block, query_n, 1, 1), NEG_FILL)
+        drop = scores - jnp.max(scores, axis=0, keepdims=True)
+        terms = jnp.exp2(drop * (scale * math.log2(math.e)))
         probs = terms * (1.0 / jnp.sum(terms, axis=0, keepdims=True))
         prob_grad = dot(value_block, grad_n, 1, 1)
         score_grad = (probs * (prob_grad - delta)).astype(jnp.bfloat16)
@@ -325,13 +333,13 @@
             for k in (2, 3):
                 block_landed(ctx_of(outer_of(o), inner_of(k)), h)
 
-    def kvg_at(e, s):
-        return kvg.at[e, :, s], kvg_recv.at[e, s]
-
-    def pass_on(s):
+    def kvg_at(e, s, h):
+        return kvg.at[e, :, s, half(h)], kvg_recv.at[e, s, h]
+
+    def pass_on(s, h):
         for e in range(1, pairs):
-            dst, recv_sem = kvg_at(e, s)
-            send(kvg_at(0, s)[0], dst, recv_sem, me, (pair + e) % pairs)
+            dst, recv_sem = kvg_at(e, s, h)
+            send(kvg_at(0, s, h)[0], dst, recv_sem, me, (pair + e) % pairs)
 
     def x_turn(chosen):
         for n, (k, e) in enumerate(slots):
@@ -354,32 +362,35 @@
         landed(g_in.at[cut], swap_recv.at[g, 1])
         if g == GROUPS // HALVES:
             wait_half(1)
-        attend(g)
         if g == 0:
             x_start(1)
+        attend(g)
         if g >= 1:
             y_start(g - 1)
         if g >= 2:
             z_start(g - 2)
     y_start(GROUPS - 1)
-    send(dq_out, dq_in, side_recv.at[1], side, pair)
     z_start(GROUPS - 2)
     z_start(GROUPS - 1)
     x_turn(0)
-    for b in range(GROUPS):
-        z_finish(b)
-    dst, recv_sem = kvg_at(0, col)
-    send(z_sum, dst, recv_sem, side, pair)
-    kvg[0, :, col] = z_sum[...]
-    pass_on(col)
+    for h in range(HALVES):
+        for b in range(h * GROUPS // HALVES, (h + 1) * GROUPS // HALVES):
+            z_finish(b)
+        dst, recv_sem = kvg_at(0, col, h)
+        send(z_sum.at[:, half(h)], dst, recv_sem, side, pair)
+        kvg[0, :, col, half(h)] = z_sum[:, half(h)]
+        pass_on(col, h)
+    send(dq_out, dq_in, side_recv.at[1], side, pair)
     x_turn(1)
-    landed(*kvg_at(0, other))
-    pass_on(other)
+    for h in range(HALVES):
+        landed(*kvg_at(0, other, h))
+        pass_on(other, h)
     landed(dq_in, side_recv.at[1])
     dq_ref[pl.ds(pl.multiple_of(other * rows, rows), rows), :] = dq_in[...]
     for e in range(1, pairs):
         for s in range(seqs):
-            landed(*kvg_at(e, s))
+            for h in range(HALVES):
+                landed(*kvg_at(e, s, h))
 
     depth = len(slots) * seqs * rows
     kv_grads = kvg[...].reshape(depth, 2 * head)
@@ -429,7 +440,8 @@
         flat = jnp.pad(flat, ((0, 0), (0, 0), (0, 0), (0, padded - width)))
     vmem = pl.BlockSpec(memory_space=pltpu.VMEM)
     both = 2 * head
-    sends = HALVES * (4 * outer + 1) + 2 * GROUPS + 2 + GROUPS * outer + 1 + 2 * (pairs - 1)
+    sends = HALVES * (4 * outer + 1) + 2 * GROUPS + 2 + GROUPS * outer
+    sends += HALVES * (1 + 2 * (pairs - 1))
     sends += (slots - 1) * x_parts + outer + (outer - 1) + (pairs - 1)
     dma = pltpu.SemaphoreType.DMA
     f32, bf16 = jnp.float32, jnp.bfloat16
@@ -477,7 +489,7 @@
             dma((HALVES, ctx)),
             dma((GROUPS,)),
             dma((GROUPS, outer - 1)),
-            dma((pairs, seqs)),
+            dma((pairs, seqs, HALVES)),
             dma((slots - 1, x_parts)),
             dma((outer,)),
             dma((outer - 1,)),

time: 51.8 us -> 51.9 us (level)
  no operation moved by 1% of the time
where the time goes in v6:
time: 51.9 us; the launch traced here: 51.7 us
  Pallas kernels  48.6 us (94%)
  local copies, waits for them, and re-layouts  2.42 us (5%)
  between operations  0.65 us (1%)
    pallas_call x1, Pallas kernels, local(): pl.pallas_call(functools.partial(kernel, (outer, pairs, width)), out_shap...  48.6 us
    unnamed x4, local copies, waits for them, and re-layouts  2.42 us

profile of v6, /device:TPU:0, one launch (start us, length us, event | category | flops | bytes accessed | tf_op | source)
XLA Modules:
  0.0 51.7 jit_solution(13158604041498525122)
XLA Ops:
  0.6 48.6 %shard_map.95 = (bf16[128,1024]{1,0:T(8,128)(2,1)}, f32[256,256]{1,0:T(8,128)}) custom-call(bf16[128,4096]{1,0:T(8,128)(2,1)} %bitcast.2, bf16[2,64,1024]{2,1,0:T(8,128)(2,1)} %q_ref.1, bf16[2,64,128]{2,1,0:T(8,128)(2,1)} %k_ref.1, bf16[2,64,128]{2,1,0:T(8,128)(2,1)} %v_ref.1, bf16[2,64,1024]{2,1,0:T(8,128)(2,1)} %a_ref.1, bf16[2,64,1024]{2,1,0:T(8,128)(2,1)} %g_ref.1, ...), custom_call_target="tpu_custom_call" | custom-call | tf_op jit(solution)/shard_map/pallas_call | solution.py:450
  49.3 0.0 copy-start
  49.3 1.7 %copy.12 = bf16[2,64,1024]{2,1,0:T(8,128)(2,1)} copy(bf16[2,64,1024]{2,1,0:T(8,128)(2,1)} %bitcast.3) | data formatting | bytes 524288
  51.0 0.0 copy-done
  51.0 0.7 %copy.13 = f32[256,256]{1,0:T(8,128)} copy(f32[256,256]{1,0:T(8,128)S(1)} %copy-done) | data formatting | bytes 524288
Async XLA Ops:
  49.3 1.7 %copy-start = (f32[256,256]{1,0:T(8,128)S(1)}, f32[256,256]{1,0:T(8,128)}, u32[]{:S(2)}) copy-start(f32[256,256]{1,0:T(8,128)} %get-tuple-element.9) | copy-start | bytes 786436

commit v7 on v6

--- a/solution.py
+++ b/solution.py
@@ -14,7 +14,7 @@
 
 
 GROUPS = 4
-HALVES = 2
+HALVES = GROUPS
 
 
 def kernel(
@@ -236,6 +236,8 @@
     forward(1)
     x_start(0)
 
+    for h in range(2, HALVES):
+        forward(h)
     own_rows = jnp.concatenate([kpos[me], kpos[side]], axis=0)
     sub = lax.broadcasted_iota(jnp.int32, own_rows.shape, 0)
     lane = lax.broadcasted_iota(jnp.int32, own_rows.shape, 1)
@@ -360,8 +362,8 @@
         cut = pl.ds(g * step, step)
         landed(q_in.at[cut], swap_recv.at[g, 0])
         landed(g_in.at[cut], swap_recv.at[g, 1])
-        if g == GROUPS // HALVES:
-            wait_half(1)
+        if g > 0:
+            wait_half(g)
         if g == 0:
             x_start(1)
         attend(g)

time: 51.9 us -> 51.7 us (level)
  no operation moved by 1% of the time
where the time goes in v7:
time: 51.7 us; the launch traced here: 51.4 us
  Pallas kernels  48.3 us (93%)
  local copies, waits for them, and re-layouts  2.42 us (5%)
  between operations  0.65 us (1%)
    pallas_call x1, Pallas kernels, local(): pl.pallas_call(functools.partial(kernel, (outer, pairs, width)), out_shap...  48.3 us
    unnamed x4, local copies, waits for them, and re-layouts  2.42 us

profile of v7, /device:TPU:0, one launch (start us, length us, event | category | flops | bytes accessed | tf_op | source)
XLA Modules:
  0.0 51.4 jit_solution(12835229048226162487)
XLA Ops:
  0.6 48.3 %shard_map.95 = (bf16[128,1024]{1,0:T(8,128)(2,1)}, f32[256,256]{1,0:T(8,128)}) custom-call(bf16[128,4096]{1,0:T(8,128)(2,1)} %bitcast.2, bf16[2,64,1024]{2,1,0:T(8,128)(2,1)} %q_ref.1, bf16[2,64,128]{2,1,0:T(8,128)(2,1)} %k_ref.1, bf16[2,64,128]{2,1,0:T(8,128)(2,1)} %v_ref.1, bf16[2,64,1024]{2,1,0:T(8,128)(2,1)} %a_ref.1, bf16[2,64,1024]{2,1,0:T(8,128)(2,1)} %g_ref.1, ...), custom_call_target="tpu_custom_call" | custom-call | tf_op jit(solution)/shard_map/pallas_call | solution.py:452
  49.0 0.0 copy-start
  49.0 1.7 %copy.12 = bf16[2,64,1024]{2,1,0:T(8,128)(2,1)} copy(bf16[2,64,1024]{2,1,0:T(8,128)(2,1)} %bitcast.3) | data formatting | bytes 524288
  50.7 0.0 copy-done
  50.7 0.7 %copy.13 = f32[256,256]{1,0:T(8,128)} copy(f32[256,256]{1,0:T(8,128)S(1)} %copy-done) | data formatting | bytes 524288
Async XLA Ops:
  49.0 1.7 %copy-start = (f32[256,256]{1,0:T(8,128)S(1)}, f32[256,256]{1,0:T(8,128)}, u32[]{:S(2)}) copy-start(f32[256,256]{1,0:T(8,128)} %get-tuple-element.9) | copy-start | bytes 786436
